TPU v7x, 512 devices: a whole 4x8x8 slice. The times are simulated.
512 devices in a mesh: dp: 16 (over z, core), expert: 8 (over y), mp: 4 (over x).
Axes of the slice: x: 4, y: 8, z: 8, core: 2. Of those that a mesh axis runs over, the one named last changes fastest.
Arguments:
- tokens: bfloat16 [16384, 2048], P(('dp', 'expert')), may hold values from -6 to 6
- out_grad: bfloat16 [16384, 2048], P(('dp', 'expert')), may hold values from -1.5 to 1.5
- routes: int32 [16384, 2], P(('dp', 'expert')), may hold values from 0 to 7, as said below
- gate_values: float32 [16384, 2], P(('dp', 'expert')), may hold values from 0.2 to 1
- gate_proj: bfloat16 [8, 704, 2048], P('expert', 'mp', 'dp'), may hold values from -0.125 to 0.125
- up_proj: bfloat16 [8, 704, 2048], P('expert', 'mp', 'dp'), may hold values from -0.125 to 0.125
- down_proj: bfloat16 [8, 704, 2048], P('expert', 'mp', 'dp'), may hold values from -0.21875 to 0.21875
Outputs:
- token_grad: bfloat16 [16384, 2048], P(('dp', 'expert'), 'mp')
- gate_grad: float32 [8, 704, 2048], P('expert', 'mp', 'dp')
- up_grad: float32 [8, 704, 2048], P('expert', 'mp', 'dp')
- down_grad: float32 [8, 704, 2048], P('expert', 'mp', 'dp')
Inputs may be any that keep to these rules, and one draw needn't show every extreme that they name: `routes`: each row names 2 different experts. In every block of 128 consecutive rows (the tokens of one device) no expert is named by more than 48 rows, and some expert, drawn afresh for each block, is named by exactly 48 rows.
All inputs are finite; a program needn't handle non-finite values.
Results may differ from a plain program's by a relative error of at most 0.02.
Values may be sent and summed in bfloat16 or wider, within the bound.
A program may use at most 64 MiB of HBM per device.

v0:
```python
import jax
import jax.numpy as jnp
from jax import lax
from jax.sharding import PartitionSpec as P


def slot_table(routes, expert_count, capacity):
    flat_ids = routes.reshape(-1)
    one_hot = (flat_ids[:, None] == jnp.arange(expert_count, dtype=jnp.int32)[None, :]).astype(
        jnp.int32
    )
    rank_in = jnp.sum(jnp.cumsum(one_hot, axis=0) * one_hot, axis=1) - 1
    return (flat_ids * capacity + rank_in, jnp.sum(one_hot, axis=0))


def pack_rows(slot_ids, rows_in, row_total):
    return jnp.zeros((row_total, rows_in.shape[1]), rows_in.dtype).at[slot_ids].set(rows_in)


def expert_terms(rows_in, rows_grad, gate_full, up_full, down_full):
    pre_gate = jnp.einsum("rd,hd->rh", rows_in, gate_full, preferred_element_type=jnp.float32)
    pre_up = jnp.einsum("rd,hd->rh", rows_in, up_full, preferred_element_type=jnp.float32)
    sigmoid_gate = jax.nn.sigmoid(pre_gate)
    active = pre_gate * sigmoid_gate
    hidden = (active * pre_up).astype(jnp.bfloat16)
    back_hidden = jnp.einsum("rd,hd->rh", rows_grad, down_full, preferred_element_type=jnp.float32)
    back_gate = (
        back_hidden * pre_up * sigmoid_gate * (1.0 + pre_gate * (1.0 - sigmoid_gate))
    ).astype(jnp.bfloat16)
    back_up = (back_hidden * active).astype(jnp.bfloat16)
    grad_gate = jnp.einsum("rh,rd->hd", back_gate, rows_in, preferred_element_type=jnp.float32)
    grad_up = jnp.einsum("rh,rd->hd", back_up, rows_in, preferred_element_type=jnp.float32)
    grad_down = jnp.einsum("rh,rd->hd", hidden, rows_grad, preferred_element_type=jnp.float32)
    row_terms = jnp.einsum("rh,hd->rd", back_gate, gate_full, preferred_element_type=jnp.float32)
    row_terms = row_terms + jnp.einsum(
        "rh,hd->rd", back_up, up_full, preferred_element_type=jnp.float32
    )
    return (grad_gate, grad_up, grad_down, row_terms)


def on_device(tokens, out_grad, routes, gate_values, gate_proj, up_proj, down_proj):
    tok_count, model_width = tokens.shape
    top_count = routes.shape[1]
    expert_count = lax.axis_size("expert")
    capacity = min(tok_count, 3 * tok_count * top_count // (2 * expert_count))
    row_total = expert_count * capacity
    slot_ids, counts = slot_table(routes, expert_count, capacity)
    copied = jnp.repeat(tokens, top_count, axis=0)
    scaled = (
        gate_values.reshape(-1, 1) * jnp.repeat(out_grad, top_count, axis=0).astype(jnp.float32)
    ).astype(jnp.bfloat16)
    gate_full, up_full, down_full = (
        lax.all_gather(gate_proj[0], "dp", axis=1, tiled=True),
        lax.all_gather(up_proj[0], "dp", axis=1, tiled=True),
        lax.all_gather(down_proj[0], "dp", axis=1, tiled=True),
    )
    slice_width = model_width // lax.axis_size("mp")
    col_start = lax.axis_index("mp") * slice_width
    recv_in, recv_grad = (
        lax.all_to_all(
            pack_rows(slot_ids, copied, row_total),
            "expert",
            split_axis=0,
            concat_axis=0,
            tiled=True,
        ),
        lax.all_to_all(
            pack_rows(slot_ids, scaled, row_total),
            "expert",
            split_axis=0,
            concat_axis=0,
            tiled=True,
        ),
    )
    grad_gate, grad_up, grad_down, row_terms = expert_terms(
        recv_in, recv_grad, gate_full, up_full, down_full
    )
    summed = lax.psum(row_terms.astype(jnp.bfloat16), "mp")
    returned = lax.all_to_all(summed, "expert", split_axis=0, concat_axis=0, tiled=True)
    returned = lax.dynamic_slice_in_dim(returned, col_start, slice_width, 1)
    picked = returned[slot_ids].astype(jnp.float32).reshape(tok_count, top_count, -1)
    token_grad = jnp.sum(picked, axis=1).astype(jnp.bfloat16)
    reduced = (
        lax.psum_scatter(
            grad_gate.astype(jnp.bfloat16), "dp", scatter_dimension=1, tiled=True
        ).astype(jnp.float32),
        lax.psum_scatter(
            grad_up.astype(jnp.bfloat16), "dp", scatter_dimension=1, tiled=True
        ).astype(jnp.float32),
        lax.psum_scatter(
            grad_down.astype(jnp.bfloat16), "dp", scatter_dimension=1, tiled=True
        ).astype(jnp.float32),
    )
    return (token_grad, reduced[0][None], reduced[1][None], reduced[2][None])


def solution(mesh):
    placed = (
        P(("dp", "expert"), None),
        P(("dp", "expert"), None),
        P(("dp", "expert"), None),
        P(("dp", "expert"), None),
        P("expert", "mp", "dp"),
        P("expert", "mp", "dp"),
        P("expert", "mp", "dp"),
    )
    return jax.shard_map(
        on_device,
        mesh=mesh,
        in_specs=placed,
        out_specs=(
            P(("dp", "expert"), "mp"),
            P("expert", "mp", "dp"),
            P("expert", "mp", "dp"),
            P("expert", "mp", "dp"),
        ),
        check_vma=False,
    )
```

profile of v0, /device:TPU:1, one launch (start us, length us, event | category | flops | bytes accessed | tf_op | source)
XLA Modules:
  0.0 335.7 jit_solution(11742089683956922533)
XLA Ops:
  11.0 1.7 broadcast_in_dim.29
  13.1 3.4 %scatter_custom_fusion.1 = bf16[384,2048]{1,0:T(8,128)(2,1)} fusion(s32[256]{0:T(256)S(1)} %bitcast.67, bf16[256,2048]{1,0:T(8,128)(2,1)S(1)} %reshape.99, bf16[]{:T(256)} %constant.9.clone.1), kind=kCustom, calls=%fused_computation.10 | custom fusion | bytes 1572866 | tf_op jit(solution)/shard_map/scatter | solution.py:17
  16.6 7.8 %all-to-all-start.1 = ((bf16[8,48,2048]{2,1,0:T(8,128)(2,1)}), bf16[8,48,2048]{2,1,0:T(8,128)(2,1)S(1)}, u32[]{:S(2)}, u32[]{:S(2)}) async-start(bf16[8,48,2048]{2,1,0:T(8,128)(2,1)} %bitcast.7), calls=%async_computation.1 | async-start | bytes 3145728 | tf_op jit(solution)/shard_map/all_to_all | solution.py:60
  24.6 2.4 broadcast_in_dim.28
  27.0 3.7 %convert_element_type.44 = f32[256,2048]{1,0:T(8,128)} reshape(f32[128,2,2048]{2,1,0:T(2,128)} %broadcast_in_dim.28) | data formatting | bytes 4194304 | tf_op jit(solution)/shard_map/convert_element_type | solution.py:50
  30.6 4.5 %scatter_custom_fusion = bf16[384,2048]{1,0:T(8,128)(2,1)} fusion(s32[256]{0:T(256)S(1)} %bitcast.68, f32[256,2048]{1,0:T(8,128)} %convert_element_type.44, f32[256]{0:T(256)S(1)} %mul.57, bf16[]{:T(256)} %constant.9.clone.1), kind=kCustom, calls=%fused_computation.8 | custom fusion | flops 1048576 | bytes 3671042 | tf_op jit(solution)/shard_map/scatter | solution.py:17
  35.2 29.6 %all-to-all-done.1 = bf16[8,48,2048]{2,1,0:T(8,128)(2,1)S(1)} async-done(((bf16[8,48,2048]{2,1,0:T(8,128)(2,1)}), bf16[8,48,2048]{2,1,0:T(8,128)(2,1)S(1)}, u32[]{:S(2)}, u32[]{:S(2)}) %all-to-all-start.1) | async-done | bytes 1572896 | tf_op jit(solution)/shard_map/all_to_all | solution.py:60
  64.8 4.4 %all-to-all-start = ((bf16[8,48,2048]{2,1,0:T(8,128)(2,1)}), bf16[8,48,2048]{2,1,0:T(8,128)(2,1)}, u32[]{:S(2)}, u32[]{:S(2)}) async-start(bf16[8,48,2048]{2,1,0:T(8,128)(2,1)} %bitcast.4), calls=%async_computation | async-start | bytes 3145728 | tf_op jit(solution)/shard_map/all_to_all | solution.py:67
  69.3 25.5 %all-gather.2 = bf16[1,176,2048]{2,1,0:T(8,128)(2,1)S(1)} all-gather(bf16[1,176,128]{2,1,0:T(8,128)(2,1)S(1)} %copy-done.2), channel_id=4, replica_groups=mesh['dp'=16,'expert'=8,'mp'=4] {'dp'}, dimensions={2}, use_global_device_ids=true | all-gather | bytes 765952 | tf_op jit(solution)/shard_map/all_gather | solution.py:53
  94.7 16.4 %all-gather.1 = bf16[1,176,2048]{2,1,0:T(8,128)(2,1)S(1)} all-gather(bf16[1,176,128]{2,1,0:T(8,128)(2,1)S(1)} %copy-done.3), channel_id=3, replica_groups=mesh['dp'=16,'expert'=8,'mp'=4] {'dp'}, dimensions={2}, use_global_device_ids=true | all-gather | bytes 765952 | tf_op jit(solution)/shard_map/all_gather | solution.py:54
  111.2 19.1 %all-gather = bf16[1,176,2048]{2,1,0:T(8,128)(2,1)} all-gather(bf16[1,176,128]{2,1,0:T(8,128)(2,1)S(1)} %copy-done.4), channel_id=2, replica_groups=mesh['dp'=16,'expert'=8,'mp'=4] {'dp'}, dimensions={2}, use_global_device_ids=true | all-gather | bytes 765952 | tf_op jit(solution)/shard_map/all_gather | solution.py:55
  131.0 1.4 fusion.10
  132.3 2.3 multiply_convert_fusion.3
  135.3 1.8 add_convert_fusion
  138.0 2.0 convolution_convert_fusion
  139.9 1.3 copy.23
  141.9 1.3 copy.19
  143.2 52.5 %all-reduce.2.cloned.1.call-done = bf16[8,48,2048]{2,1,0:T(8,128)(2,1)} async-done(((bf16[8,48,2048]{2,1,0:T(8,128)(2,1)}), bf16[8,48,2048]{2,1,0:T(8,128)(2,1)}) %all-reduce.2.cloned.1.call-update) | async-done | bytes 1572880 | tf_op jit(solution)/shard_map/psum | solution.py:78
  195.7 6.5 %all-to-all-start.2 = ((bf16[8,48,2048]{2,1,0:T(8,128)(2,1)}), bf16[8,48,2048]{2,1,0:T(8,128)(2,1)}, u32[]{:S(2)}, u32[]{:S(2)}) async-start(bf16[8,48,2048]{2,1,0:T(8,128)(2,1)} %all-reduce.2.cloned.1.call-done), calls=%async_computation.2 | async-start | bytes 3145728 | tf_op jit(solution)/shard_map/all_to_all | solution.py:79
  202.8 1.3 copy.21
  205.1 55.7 %reduce-scatter.10.cloned.1.call-done = bf16[128,176]{1,0:T(8,128)(2,1)} async-done(((bf16[2048,176]{1,0:T(8,128)(2,1)}), bf16[128,176]{1,0:T(8,128)(2,1)}) %reduce-scatter.10.cloned.1.call-update) | async-done | bytes 45072
  261.8 59.8 %reduce-scatter.12.cloned.1.call-done = bf16[128,176]{1,0:T(8,128)(2,1)} async-done(((bf16[2048,176]{1,0:T(8,128)(2,1)}), bf16[128,176]{1,0:T(8,128)(2,1)}) %reduce-scatter.12.cloned.1.call-update) | async-done | bytes 45072
  325.5 1.2 gather_fusion
  326.7 1.3 reduce_sum.22
  (57 shorter events, 13.1 us)
Async XLA Ops:
  13.1 17.5 %copy-start.5 = (s32[256,1]{0,1:T(1,128)}, s32[256,1]{0,1:T(1,128)S(1)}, u32[]{:S(2)}) copy-start(s32[256,1]{0,1:T(1,128)S(1)} %compare_select_fusion) | copy-start | bytes 3076
  16.5 7.8 %copy-start.7 = (f32[128,2]{0,1:T(2,128)S(1)}, f32[128,2]{0,1:T(2,128)}, u32[]{:S(2)}) copy-start(f32[128,2]{0,1:T(2,128)} %param.10) | copy-start | bytes 3076
  16.5 8.0 %copy-start = (bf16[128,2048]{1,0:T(8,128)(2,1)S(1)}, bf16[128,2048]{1,0:T(8,128)(2,1)}, u32[]{:S(2)}) copy-start(bf16[128,2048]{1,0:T(8,128)(2,1)} %param.8) | copy-start | bytes 1572868
  16.6 48.2 %all-to-all-start.1 = ((bf16[8,48,2048]{2,1,0:T(8,128)(2,1)}), bf16[8,48,2048]{2,1,0:T(8,128)(2,1)S(1)}, u32[]{:S(2)}, u32[]{:S(2)}) async-start(bf16[8,48,2048]{2,1,0:T(8,128)(2,1)} %bitcast.7), calls=%async_computation.1 | async-start | bytes 3145728 | tf_op jit(solution)/shard_map/all_to_all | solution.py:60
  64.8 4.5 %copy-start.2 = (bf16[1,176,128]{2,1,0:T(8,128)(2,1)S(1)}, bf16[1,176,128]{2,1,0:T(8,128)(2,1)}, u32[]{:S(2)}) copy-start(bf16[1,176,128]{2,1,0:T(8,128)(2,1)} %param.11) | copy-start | bytes 135172
  64.8 30.0 %copy-start.3 = (bf16[1,176,128]{2,1,0:T(8,128)(2,1)S(1)}, bf16[1,176,128]{2,1,0:T(8,128)(2,1)}, u32[]{:S(2)}) copy-start(bf16[1,176,128]{2,1,0:T(8,128)(2,1)} %param.12) | copy-start | bytes 135172
  64.8 46.4 %copy-start.4 = (bf16[1,176,128]{2,1,0:T(8,128)(2,1)S(1)}, bf16[1,176,128]{2,1,0:T(8,128)(2,1)}, u32[]{:S(2)}) copy-start(bf16[1,176,128]{2,1,0:T(8,128)(2,1)} %param.13) | copy-start | bytes 135172
  64.8 67.6 %all-to-all-start = ((bf16[8,48,2048]{2,1,0:T(8,128)(2,1)}), bf16[8,48,2048]{2,1,0:T(8,128)(2,1)}, u32[]{:S(2)}, u32[]{:S(2)}) async-start(bf16[8,48,2048]{2,1,0:T(8,128)(2,1)} %bitcast.4), calls=%async_computation | async-start | bytes 3145728 | tf_op jit(solution)/shard_map/all_to_all | solution.py:67
  69.2 126.5 %all-reduce.2.cloned.1.call-start = ((), (), s32[]{:S(2)}) async-start(), calls=%async_computation.6 | async-start | bytes 3145728 | tf_op jit(solution)/shard_map/psum | solution.py:78
  137.0 1.0 copy-start.1
  137.1 67.1 %reduce-scatter.14.cloned.1.call-start = ((), (), s32[]{:S(2)}) async-start(), calls=%async_computation.9 | async-start | bytes 1114112
  141.3 119.6 %reduce-scatter.10.cloned.1.call-start = ((), (), s32[]{:S(2)}) async-start(), calls=%async_computation.7 | async-start | bytes 1114112
  195.7 128.8 %all-to-all-start.2 = ((bf16[8,48,2048]{2,1,0:T(8,128)(2,1)}), bf16[8,48,2048]{2,1,0:T(8,128)(2,1)}, u32[]{:S(2)}, u32[]{:S(2)}) async-start(bf16[8,48,2048]{2,1,0:T(8,128)(2,1)} %all-reduce.2.cloned.1.call-done), calls=%async_computation.2 | async-start | bytes 3145728 | tf_op jit(solution)/shard_map/all_to_all | solution.py:79
  202.2 119.4 %reduce-scatter.12.cloned.1.call-start = ((), (), s32[]{:S(2)}) async-start(), calls=%async_computation.8 | async-start | bytes 1114112
  202.8 1.4 copy-start.6
Sparse Core Ops, SparseCore 0:
  137.2 58.4 all-reduce.1
Sparse Core Ops, SparseCore 1:
  141.4 56.5 reduce-scatter.13
  200.9 59.9 reduce-scatter.9
  263.5 58.0 reduce-scatter.11
where the time goes:
time: 338 us; the launch traced here: 336 us
  waiting for transfers between devices  198 us (59%)
  blocking collectives  61 us (18%)
  local copies, waits for them, and re-layouts  23.1 us (7%)
  starting transfers between devices  19 us (6%)
  between operations  15.8 us (5%)
  matrix products  9.76 us (3%)
  other arithmetic  9.22 us (3%)
    unnamed x7, waiting for transfers between devices  116 us
    psum x1, waiting for transfers between devices, on_device(): summed = lax.psum(row_terms.astype(jnp.bfloat16), 'mp')  52.5 us
    all_to_all x1, waiting for transfers between devices, on_device(): lax.all_to_all(pack_rows(slot_ids, copied, row_total), 'expert', split_ax...  29.6 us
    all_gather x1, blocking collectives, on_device(): lax.all_gather(gate_proj[0], 'dp', axis=1, tiled=True)  25.5 us
    all_gather x1, blocking collectives, on_device(): lax.all_gather(down_proj[0], 'dp', axis=1, tiled=True)  19.1 us
    all_gather x1, blocking collectives, on_device(): lax.all_gather(up_proj[0], 'dp', axis=1, tiled=True)  16.4 us
    unnamed x24, local copies, waits for them, and re-layouts  8.37 us
    all_to_all x1, starting transfers between devices, on_device(): lax.all_to_all(pack_rows(slot_ids, copied, row_total), 'expert', split_ax...  7.78 us
  transfers between devices with their start and end apart: 7, of which 4 were waited for; matrix products, arithmetic and copies ran while one was open for 7% of the time, Pallas kernels for 0%

commit v1 on v0

v1 whole, which is shorter than its diff:
```python
import functools

import jax
import jax.numpy as jnp
from jax import lax
from jax.experimental import pallas as pl
from jax.experimental.pallas import tpu as pltpu
from jax.sharding import PartitionSpec as P

MESH = pl.DeviceIdType.MESH
F32 = jnp.float32
BF16 = jnp.bfloat16

SHIFTS = (0, 1, 7, 2, 6, 3, 5, 4)
SLOTS = 8
CAP = 48
HID = 176
HID3 = 3 * HID
CUT = 272
PIECES = ((0, CUT), (CUT, HID3 - CUT))


def dot(a, b, ca, cb):
    return lax.dot_general(a, b, (((ca,), (cb,)), ((), ())), preferred_element_type=F32)


def kernel(
    tok_hbm, grad_hbm, routes_ref, gates_ref, gate_hbm, up_hbm, down_hbm,
    tok_out, gate_out, up_out, down_out,
    tokq, gradq, pack, sendq, rows, weights, back, hid, row_grad, wgrad, sib_rs, ring_in, ring_out, xs_in, yback, ret,
    loc, y_s, y_r, x_s, x_r, ag_s, ag_r, sg_s, sg_r, xs_s, xs_r, yb_s, yb_r, sr_s, sr_r, rr_s, rr_r,
):
    d, e, m = lax.axis_index("dp"), lax.axis_index("expert"), lax.axis_index("mp")
    z, c = d // 2, d % 2
    width = tokq.shape[1]

    def at_z(shift, core=None):
        return ((((z + shift) % 8) * 2 + (c if core is None else core)), e, m)

    def at_y(shift):
        return (d, (e + shift) % 8, m)

    def at_x(shift):
        return (d, e, (m + shift) % 4)

    z_right, z_left, sibling = at_z(1), at_z(7), at_z(0, 1 - c)
    x_right, x_left, x_far = at_x(1), at_x(3), at_x(2)

    def quarter(shift):
        return pl.ds(pl.multiple_of(((m + shift) % 4) * width, width), width)

    def block(shift, core):
        return pl.ds(pl.multiple_of((((z + shift) % 8) * 2 + core) * 128, 128), 128)

    def remote(src, dst, send, recv, device):
        return pltpu.make_async_remote_copy(
            src_ref=src, dst_ref=dst, send_sem=send, recv_sem=recv, device_id=device, device_id_type=MESH
        )

    pending = []

    def send(src, dst, send_sem, recv_sem, device):
        copy = remote(src, dst, send_sem, recv_sem, device)
        copy.start()
        pending.append(copy)

    def arrived(dst, send_sem, recv_sem, device):
        remote(dst, dst, send_sem, recv_sem, device).wait_recv()

    barrier = pltpu.get_barrier_semaphore()
    partners = [z_right, z_left, sibling, x_right, x_left, x_far] + [at_y(k) for k in range(1, 8)]
    for partner in partners:
        pl.semaphore_signal(barrier, inc=1, device_id=partner, device_id_type=MESH)

    own = block(0, c)
    loads = [
        pltpu.make_async_copy(tok_hbm.at[:, quarter(0)], tokq, loc.at[0]),
        pltpu.make_async_copy(grad_hbm.at[:, quarter(0)], gradq, loc.at[1]),
        pltpu.make_async_copy(gate_hbm.at[0], weights.at[pl.ds(0, HID), own], loc.at[2]),
        pltpu.make_async_copy(up_hbm.at[0], weights.at[pl.ds(HID, HID), own], loc.at[3]),
        pltpu.make_async_copy(down_hbm.at[0], weights.at[pl.ds(2 * HID, HID), own], loc.at[4]),
    ]
    for copy in loads:
        copy.start()

    count = tokq.shape[0]
    slot_id = lax.broadcasted_iota(jnp.int32, (SLOTS, count), 0)
    wanted = jnp.zeros((SLOTS, count), jnp.int32)
    for j, shift in enumerate(SHIFTS):
        wanted = jnp.where(slot_id == j, (e + shift) % 8, wanted)
    first = routes_ref[0:1, :] == wanted
    second = routes_ref[1:2, :] == wanted
    named = jnp.where(first, 1.0, jnp.where(second, 1.0, 0.0))
    value = jnp.where(first, gates_ref[0:1, :], jnp.where(second, gates_ref[1:2, :], 0.0))
    earlier = jnp.where(
        lax.broadcasted_iota(jnp.int32, (count, count), 0) < lax.broadcasted_iota(jnp.int32, (count, count), 1),
        1.0, 0.0,
    ).astype(BF16)
    rank = dot(named.astype(BF16), earlier, 1, 0).astype(jnp.int32)
    place = jnp.where(named > 0.5, rank, -1)
    row_id = lax.broadcasted_iota(jnp.int32, (CAP, count), 0)
    scales = []
    for j in range(SLOTS):
        taken = place[j : j + 1, :] == row_id
        pack[pl.ds(j * CAP, CAP), :] = jnp.where(taken, 1.0, 0.0).astype(BF16)
        scales.append(jnp.sum(jnp.where(taken, value[j : j + 1, :], 0.0), axis=1, keepdims=True))

    loads[0].wait()
    loads[1].wait()

    def pack_slots(lo, hi):
        chosen = pack[pl.ds(lo * CAP, (hi - lo) * CAP), :]
        taken_rows = dot(chosen, tokq[...], 1, 0).astype(BF16)
        taken_grads = dot(chosen, gradq[...], 1, 0)
        for j in range(lo, hi):
            part = slice((j - lo) * CAP, (j - lo + 1) * CAP)
            sendq[j, 0:CAP, :] = taken_rows[part]
            sendq[j, CAP : 2 * CAP, :] = (taken_grads[part] * scales[j]).astype(BF16)

    def y_send(j):
        send(sendq.at[j], rows.at[j, :, quarter(0)], y_s.at[j], y_r.at[j], at_y(SHIFTS[j]))

    def x_send(j):
        src = sendq.at[0] if j == 0 else rows.at[j, :, quarter(0)]
        send(src, rows.at[j, :, quarter(0)], x_s.at[j, 0], x_r.at[j, 0], x_right)
        send(src, rows.at[j, :, quarter(0)], x_s.at[j, 1], x_r.at[j, 1], x_left)

    def x_forward(j):
        arrived(rows.at[j, :, quarter(3)], x_s.at[j, 0], x_r.at[j, 0], x_left)
        part = rows.at[j, pl.ds(0, CAP), quarter(3)]
        send(part, part, x_s.at[j, 2], x_r.at[j, 2], x_right)
        arrived(rows.at[j, :, quarter(1)], x_s.at[j, 1], x_r.at[j, 1], x_right)
        part = rows.at[j, pl.ds(CAP, CAP), quarter(1)]
        send(part, part, x_s.at[j, 3], x_r.at[j, 3], x_left)

    def x_complete(j):
        arrived(rows.at[j, pl.ds(0, CAP), quarter(2)], x_s.at[j, 2], x_r.at[j, 2], x_left)
        arrived(rows.at[j, pl.ds(CAP, CAP), quarter(2)], x_s.at[j, 3], x_r.at[j, 3], x_right)

    def weight_part(shift, core, half):
        if half is None:
            return weights.at[:, block(shift, core)]
        return weights.at[pl.ds(*PIECES[half]), block(shift, core)]

    def ag_send(step, side):
        shift = (8 - (step - 1)) % 8 if side == 0 else step - 1
        part = weight_part(shift, c, side if step == 4 else None)
        send(part, part, ag_s.at[side, step - 1], ag_r.at[side, step - 1], z_right if side == 0 else z_left)

    def sib_send(index, shift, half=None):
        part = weight_part(shift, c, half)
        send(part, part, sg_s.at[index], sg_r.at[index], sibling)

    def ag_step(step):
        for side in (0, 1):
            shift = 8 - step if side == 0 else step
            half = side if step == 4 else None
            arrived(
                weight_part(shift, c, half), ag_s.at[side, step - 1], ag_r.at[side, step - 1],
                z_left if side == 0 else z_right,
            )
            if step < 4:
                ag_send(step + 1, side)
            sib_send(1 + 2 * (step - 1) + side, shift, half)

    def weights_complete():
        arrived(weight_part(0, 1 - c, None), sg_s.at[0], sg_r.at[0], sibling)
        for step in range(1, 5):
            for side in (0, 1):
                shift = 8 - step if side == 0 else step
                half = side if step == 4 else None
                index = 1 + 2 * (step - 1) + side
                arrived(weight_part(shift, 1 - c, half), sg_s.at[index], sg_r.at[index], sibling)

    def batch(b, lo, lanes=slice(None)):
        part = rows[4 * b : 4 * b + 4, lo : lo + CAP, lanes]
        return part.reshape(4 * CAP, part.shape[2])

    def forward(b):
        pre = dot(weights[0 : 2 * HID, :], batch(b, 0), 1, 1)
        back_hidden = dot(weights[2 * HID : HID3, :], batch(b, CAP), 1, 1)
        pre_gate, pre_up = pre[0:HID], pre[HID : 2 * HID]
        s = jax.nn.sigmoid(pre_gate)
        active = pre_gate * s
        hid[b] = (active * pre_up).astype(BF16)
        back[b, 0:HID] = (back_hidden * pre_up * s * (1.0 + pre_gate * (1.0 - s))).astype(BF16)
        back[b, HID : 2 * HID] = (back_hidden * active).astype(BF16)

    def row_grads(b):
        for q in range(4):
            lanes = slice(q * width, (q + 1) * width)
            part = dot(back[b], weights[0 : 2 * HID, lanes], 0, 0).astype(BF16)
            row_grad[4 * b : 4 * b + 4, :, lanes] = part.reshape(4, CAP, width)

    def rs_send(j):
        for index, (shift, device) in enumerate(((1, x_right), (3, x_left), (2, x_far))):
            send(
                row_grad.at[j, :, quarter(shift)], xs_in.at[j, index], xs_s.at[j, index], xs_r.at[j, index], device,
            )

    def rs_finish(j):
        total = row_grad[j, :, quarter(0)].astype(F32)
        for index, device in enumerate((x_left, x_right, x_far)):
            arrived(xs_in.at[j, index], xs_s.at[j, index], xs_r.at[j, index], device)
            total = total + xs_in[j, index].astype(F32)
        if j == 0:
            ret[0] = total.astype(BF16)
        else:
            yback[j] = total.astype(BF16)
            send(yback.at[j], ret.at[j], yb_s.at[j], yb_r.at[j], at_y(8 - SHIFTS[j]))

    def weight_chunk(index, shift):
        lanes = pl.ds(pl.multiple_of(((z + shift) % 8) * 256, 256), 256)
        grad_gu = dot(back[0], batch(0, 0, lanes), 1, 0) + dot(back[1], batch(1, 0, lanes), 1, 0)
        grad_d = dot(hid[0], batch(0, CAP, lanes), 1, 0) + dot(hid[1], batch(1, CAP, lanes), 1, 0)
        wgrad[0 : 2 * HID, lanes] = grad_gu.astype(BF16)
        wgrad[2 * HID : HID3, lanes] = grad_d.astype(BF16)
        send(wgrad.at[:, block(shift, 1 - c)], sib_rs.at[index], sr_s.at[index], sr_r.at[index], sibling)

    chunk_shifts = (4, 3, 5, 2, 6, 1, 7, 0)

    def pair_ready(index):
        arrived(sib_rs.at[index], sr_s.at[index], sr_r.at[index], sibling)

    def pair_sum(index, lo, size):
        mine = wgrad[pl.ds(lo, size), block(chunk_shifts[index], c)].astype(F32)
        return mine + sib_rs[index, pl.ds(lo, size), :].astype(F32)

    def ring_part(ref, side, step, piece):
        return ref.at[side, step - 1, pl.ds(*PIECES[piece])]

    def ring_send(step, side, piece, total):
        lo, size = PIECES[piece]
        ring_out[side, step - 1, pl.ds(lo, size), :] = total.astype(BF16)
        send(
            ring_part(ring_out, side, step, piece), ring_part(ring_in, side, step, piece),
            rr_s.at[side, step - 1, piece], rr_r.at[side, step - 1, piece], z_right if side == 0 else z_left,
        )

    def ring_recv(step, side, piece):
        lo, size = PIECES[piece]
        arrived(
            ring_part(ring_in, side, step, piece), rr_s.at[side, step - 1, piece], rr_r.at[side, step - 1, piece],
            z_left if side == 0 else z_right,
        )
        return ring_in[side, step - 1, pl.ds(lo, size), :].astype(F32)

    def ring_step(step):
        if step == 1:
            pair_ready(0)
            for side in (0, 1):
                ring_send(1, side, side, pair_sum(0, *PIECES[side]))
            return
        for side in (0, 1):
            pair_ready(2 * step - 3 + side)
        for turn in (0, 1):
            for side in (0, 1):
                piece = side if turn == 0 else 1 - side
                total = pair_sum(2 * step - 3 + side, *PIECES[piece])
                if step > 2 or piece == side:
                    total = total + ring_recv(step - 1, side, piece)
                ring_send(step, side, piece, total)

    pack_slots(0, 4)
    for copy in loads[2:]:
        copy.wait()
    pl.semaphore_wait(barrier, len(partners))

    for j in (1, 2, 3, 4):
        if j == 4:
            pack_slots(4, 8)
        y_send(j)
    x_send(0)
    keep = pltpu.make_async_copy(sendq.at[0], rows.at[0, :, quarter(0)], loc.at[5])
    keep.start()
    ag_send(1, 0)
    ag_send(1, 1)
    sib_send(0, 0)

    for i in range(1, 9):
        if i < 8:
            arrived(rows.at[i, :, quarter(0)], y_s.at[i], y_r.at[i], at_y(8 - SHIFTS[i]))
            x_send(i)
            if i + 4 < 8:
                y_send(i + 4)
        x_forward(i - 1)
        if i <= 4:
            ag_step(i)
        if i >= 2:
            x_complete(i - 2)
        if i == 6:
            keep.wait()
            weights_complete()
            forward(0)
        if i == 7:
            row_grads(0)
    for j in (0, 1, 2, 3):
        rs_send(j)
    x_complete(7)

    forward(1)
    for index, shift in enumerate(chunk_shifts):
        weight_chunk(index, shift)
        if index == 2:
            ring_step(1)
    row_grads(1)
    for j in (7, 6, 5, 4):
        rs_send(j)
    rs_finish(0)
    rs_finish(1)
    ring_step(2)
    rs_finish(2)
    rs_finish(3)
    ring_step(3)
    rs_finish(7)
    rs_finish(6)
    ring_step(4)
    rs_finish(5)
    rs_finish(4)
    for j in range(1, SLOTS):
        arrived(ret.at[j], yb_s.at[j], yb_r.at[j], at_y(SHIFTS[j]))
    back_rows = ret[...].reshape(SLOTS * CAP, width)
    tok_out[...] = dot(pack[...], back_rows, 0, 0).astype(BF16)

    pair_ready(7)
    totals = []
    for piece in (0, 1):
        totals.append(pair_sum(7, *PIECES[piece]) + ring_recv(4, 0, piece) + ring_recv(4, 1, piece))
    gate_out[0] = totals[0][0:HID]
    up_out[0, 0 : CUT - HID] = totals[0][HID:CUT]
    up_out[0, CUT - HID : HID] = totals[1][0 : 2 * HID - CUT]
    down_out[0] = totals[1][2 * HID - CUT :]

    for copy in pending:
        copy.wait_send()


def on_device(tokens, out_grad, routes, gate_values, gate_proj, up_proj, down_proj):
    count, model = tokens.shape
    width = model // lax.axis_size("mp")
    sems = pltpu.SemaphoreType.DMA
    vmem = pl.BlockSpec(memory_space=pltpu.VMEM)
    hbm = pl.BlockSpec(memory_space=pl.ANY)
    weight_out = jax.ShapeDtypeStruct(gate_proj.shape, F32)
    return pl.pallas_call(
        kernel,
        out_shape=(jax.ShapeDtypeStruct((count, width), BF16), weight_out, weight_out, weight_out),
        in_specs=[hbm, hbm, vmem, vmem, hbm, hbm, hbm],
        out_specs=(vmem, vmem, vmem, vmem),
        scratch_shapes=[
            pltpu.VMEM((count, width), BF16),
            pltpu.VMEM((count, width), BF16),
            pltpu.VMEM((SLOTS * CAP, count), BF16),
            pltpu.VMEM((SLOTS, 2 * CAP, width), BF16),
            pltpu.VMEM((SLOTS, 2 * CAP, model), BF16),
            pltpu.VMEM((HID3, model), BF16),
            pltpu.VMEM((2, 2 * HID, 4 * CAP), BF16),
            pltpu.VMEM((2, HID, 4 * CAP), BF16),
            pltpu.VMEM((SLOTS, CAP, model), BF16),
            pltpu.VMEM((HID3, model), BF16),
            pltpu.VMEM((8, HID3, 128), BF16),
            pltpu.VMEM((2, 4, HID3, 128), BF16),
            pltpu.VMEM((2, 4, HID3, 128), BF16),
            pltpu.VMEM((SLOTS, 3, CAP, width), BF16),
            pltpu.VMEM((SLOTS, CAP, width), BF16),
            pltpu.VMEM((SLOTS, CAP, width), BF16),
            sems((6,)),
            sems((SLOTS,)),
            sems((SLOTS,)),
            sems((SLOTS, 4)),
            sems((SLOTS, 4)),
            sems((2, 4)),
            sems((2, 4)),
            sems((9,)),
            sems((9,)),
            sems((SLOTS, 3)),
            sems((SLOTS, 3)),
            sems((SLOTS,)),
            sems((SLOTS,)),
            sems((8,)),
            sems((8,)),
            sems((2, 4, 2)),
            sems((2, 4, 2)),
        ],
        compiler_params=pltpu.CompilerParams(
            collective_id=0, has_side_effects=True, vmem_limit_bytes=40 * 1024 * 1024
        ),
        cost_estimate=pl.CostEstimate(flops=2300000000, bytes_accessed=4000000, transcendentals=70000),
        name="experts",
    )(tokens, out_grad, routes.T, gate_values.T, gate_proj, up_proj, down_proj)


def solution(mesh):
    tokens_in = P(("dp", "expert"), None)
    weights_in = P("expert", "mp", "dp")
    return jax.shard_map(
        on_device,
        mesh=mesh,
        in_specs=(tokens_in, tokens_in, tokens_in, tokens_in, weights_in, weights_in, weights_in),
        out_specs=(P(("dp", "expert"), "mp"), weights_in, weights_in, weights_in),
        check_vma=False,
    )
```

time: 338 us -> 82.7 us (0.24)
  waiting for transfers between devices: 198 us -> 0 us
  Pallas kernels: 0 us -> 73.8 us
  blocking collectives: 61 us -> 0 us
  starting transfers between devices: 19 us -> 0 us
  local copies, waits for them, and re-layouts: 23.1 us -> 7.7 us
  between operations: 15.8 us -> 0.66 us
  matrix products: 9.76 us -> 0 us
  other arithmetic: 9.22 us -> 0 us
    unnamed x7 -> x0, waiting for transfers between devices: 116 us -> none
    pallas_call x0 -> x1, Pallas kernels: none -> 73.8 us  [on_device(): pl.pallas_call(kernel, out_shape=(jax.ShapeDtypeStruct((count, width), BF...]
    all_gather x3 -> x0, blocking collectives: 61 us -> none  [the longest x1 25.5 us: on_device(): lax.all_gather(gate_proj[0], 'dp', axis=1, tiled=True)]
    psum x1 -> x0, waiting for transfers between devices: 52.5 us -> none  [on_device(): summed = lax.psum(row_terms.astype(jnp.bfloat16), 'mp')]
    all_to_all x3 -> x0, waiting for transfers between devices: 29.6 us -> none  [the longest x1 29.6 us: on_device(): lax.all_to_all(pack_rows(slot_ids, copied, row_total), 'expert', split_ax...]
    all_to_all x3 -> x0, starting transfers between devices: 18.7 us -> none  [the longest x1 7.78 us: on_device(): lax.all_to_all(pack_rows(slot_ids, copied, row_total), 'expert', split_ax...]
    dot_general x8 -> x0, matrix products: 9.76 us -> none  [the longest x1 2.32 us: expert_terms(): jnp.einsum('rd,hd->rh', rows_grad, down_full, preferred_element_type=jnp....]
    scatter x1 -> x0, other arithmetic: 4.53 us -> none  [pack_rows(): jnp.zeros((row_total, rows_in.shape[1]), rows_in.dtype).at[slot_ids]]
  transfers between devices with their start and end apart: 7 -> 0, of which waited for: 4 -> 0; matrix products, arithmetic and copies ran while one was open for 7% -> 0% of each run, Pallas kernels for 0% -> 0%
where the time goes in v1:
time: 82.7 us; the launch traced here: 82.2 us
  Pallas kernels  73.8 us (89%)
  local copies, waits for them, and re-layouts  7.7 us (9%)
    pallas_call x1, Pallas kernels, on_device(): pl.pallas_call(kernel, out_shape=(jax.ShapeDtypeStruct((count, width), BF...  73.8 us
    unnamed x18, local copies, waits for them, and re-layouts  7.7 us

profile of v1, /device:TPU:1, one launch (start us, length us, event | category | flops | bytes accessed | tf_op | source)
XLA Modules:
  0.0 82.2 jit_solution(16483301496937125126)
XLA Ops:
  0.6 0.0 copy-start.6
  0.6 0.0 copy-start.5
  0.7 0.7 copy-done.6
  1.3 0.0 copy-done.5
  1.3 0.0 copy-start
  1.3 1.0 %copy-done = bf16[128,2048]{1,0:T(8,128)(2,1)S(1)} copy-done((bf16[128,2048]{1,0:T(8,128)(2,1)S(1)}, bf16[128,2048]{1,0:T(8,128)(2,1)}, u32[]{:S(2)}) %copy-start) | copy-done | bytes 524312
  2.4 0.0 copy-start.1
  2.4 1.0 %copy-done.1 = bf16[128,2048]{1,0:T(8,128)(2,1)S(1)} copy-done((bf16[128,2048]{1,0:T(8,128)(2,1)S(1)}, bf16[128,2048]{1,0:T(8,128)(2,1)}, u32[]{:S(2)}) %copy-start.1) | copy-done | bytes 524312
  3.4 0.0 copy-start.2
  3.4 0.8 copy-done.2
  4.2 0.0 copy-start.3
  4.2 0.8 copy-done.3
  5.0 0.0 copy-start.4
  5.0 0.8 copy-done.4
  5.8 73.8 %experts.1 = (bf16[128,512]{1,0:T(8,128)(2,1)S(1)}, f32[1,176,128]{2,1,0:T(8,128)S(1)}, f32[1,176,128]{2,1,0:T(8,128)S(1)}, f32[1,176,128]{2,1,0:T(8,128)S(1)}) custom-call(bf16[128,2048]{1,0:T(8,128)(2,1)S(1)} %copy-done, bf16[128,2048]{1,0:T(8,128)(2,1)S(1)} %copy-done.1, s32[2,128]{1,0:T(2,128)S(1)} %bitcast.2, f32[2,128]{1,0:T(2,128)S(1)} %bitcast.3, ...), custom_call_target="tpu_custom_call" | custom-call | flops 2300000000 | bytes 4000000 | tf_op jit(solution)/shard_map/experts/pallas_call | solution.py:345
  79.6 0.7 copy.15
  80.2 0.6 copy.16
  80.9 0.6 copy.17
  81.5 0.6 copy.18
Async XLA Ops:
  0.6 0.7 copy-start.6
  0.6 0.7 copy-start.5
  1.3 1.0 %copy-start = (bf16[128,2048]{1,0:T(8,128)(2,1)S(1)}, bf16[128,2048]{1,0:T(8,128)(2,1)}, u32[]{:S(2)}) copy-start(bf16[128,2048]{1,0:T(8,128)(2,1)} %tok_hbm.1) | copy-start | bytes 1572868
  2.4 1.0 %copy-start.1 = (bf16[128,2048]{1,0:T(8,128)(2,1)S(1)}, bf16[128,2048]{1,0:T(8,128)(2,1)}, u32[]{:S(2)}) copy-start(bf16[128,2048]{1,0:T(8,128)(2,1)} %grad_hbm.1) | copy-start | bytes 1572868
  3.4 0.8 copy-start.2
  4.2 0.8 copy-start.3
  5.0 0.8 copy-start.4

commit v2 on v1

v2 whole, which is shorter than its diff:
```python
import functools

import jax
import jax.numpy as jnp
from jax import lax
from jax.experimental import pallas as pl
from jax.experimental.pallas import tpu as pltpu
from jax.sharding import PartitionSpec as P

MESH = pl.DeviceIdType.MESH
F32 = jnp.float32
BF16 = jnp.bfloat16

SHIFTS = (0, 2, 6, 3, 5, 4, 1, 7)
SLOTS = 8
FAR = 6
NEAR = (6, 7)
BATCHES = ((0, 3), (3, 8))
CAP = 48
HID = 176
HID3 = 3 * HID
HALVES = ((0, 272), (272, 256))
PIECES = ((0, 144), (144, 128), (272, 128), (400, 128))


def dot(a, b, ca, cb):
    return lax.dot_general(a, b, (((ca,), (cb,)), ((), ())), preferred_element_type=F32)


def kernel(
    tok_hbm, grad_hbm, routes_hbm, gates_hbm, gate_hbm, up_hbm, down_hbm,
    tok_out, gate_out, up_out, down_out,
    tokq, gradq, tokf, gradf, routes_ref, gates_ref, pack, sendq, sendf, rows, weights, back_a, back_b, hid_a, hid_b,
    row_grad, wacc, wgrad, sib_rs, ring_in, ring_out, xs_in, yback, ret,
    loc, y_s, y_r, x_s, x_r, ag_s, ag_r, sg_s, sg_r, xs_s, xs_r, yb_s, yb_r, sr_s, sr_r, rr_s, rr_r,
):
    d, e, m = lax.axis_index("dp"), lax.axis_index("expert"), lax.axis_index("mp")
    z, c = d // 2, d % 2
    width = tokq.shape[1]

    def at_z(shift, core=None):
        return ((((z + shift) % 8) * 2 + (c if core is None else core)), e, m)

    def at_y(shift):
        return (d, (e + shift) % 8, m)

    def at_x(shift):
        return (d, e, (m + shift) % 4)

    z_right, z_left, sibling = at_z(1), at_z(7), at_z(0, 1 - c)
    x_right, x_left, x_far = at_x(1), at_x(3), at_x(2)

    def quarter(shift):
        return pl.ds(pl.multiple_of(((m + shift) % 4) * width, width), width)

    def block(shift, core):
        return pl.ds(pl.multiple_of((((z + shift) % 8) * 2 + core) * 128, 128), 128)

    def remote(src, dst, send, recv, device):
        return pltpu.make_async_remote_copy(
            src_ref=src, dst_ref=dst, send_sem=send, recv_sem=recv, device_id=device, device_id_type=MESH
        )

    pending = []

    def send(src, dst, send_sem, recv_sem, device):
        copy = remote(src, dst, send_sem, recv_sem, device)
        copy.start()
        pending.append(copy)

    def arrived(dst, send_sem, recv_sem, device):
        remote(dst, dst, send_sem, recv_sem, device).wait_recv()

    barrier = pltpu.get_barrier_semaphore()
    partners = [z_right, z_left, sibling, x_right, x_left, x_far] + [at_y(k) for k in range(1, 8)]
    for partner in partners:
        pl.semaphore_signal(barrier, inc=1, device_id=partner, device_id_type=MESH)

    own = block(0, c)
    loads = [
        pltpu.make_async_copy(routes_hbm, routes_ref, loc.at[0]),
        pltpu.make_async_copy(gates_hbm, gates_ref, loc.at[1]),
        pltpu.make_async_copy(tok_hbm.at[:, quarter(0)], tokq, loc.at[2]),
        pltpu.make_async_copy(grad_hbm.at[:, quarter(0)], gradq, loc.at[3]),
        pltpu.make_async_copy(gate_hbm.at[0], weights.at[pl.ds(0, HID), own], loc.at[4]),
        pltpu.make_async_copy(up_hbm.at[0], weights.at[pl.ds(HID, HID), own], loc.at[5]),
        pltpu.make_async_copy(down_hbm.at[0], weights.at[pl.ds(2 * HID, HID), own], loc.at[6]),
        pltpu.make_async_copy(tok_hbm, tokf, loc.at[7]),
        pltpu.make_async_copy(grad_hbm, gradf, loc.at[8]),
    ]
    for copy in loads:
        copy.start()

    loads[0].wait()
    loads[1].wait()
    count = tokq.shape[0]
    slot_id = lax.broadcasted_iota(jnp.int32, (SLOTS, count), 0)
    wanted = jnp.zeros((SLOTS, count), jnp.int32)
    for j, shift in enumerate(SHIFTS):
        wanted = jnp.where(slot_id == j, (e + shift) % 8, wanted)
    first = routes_ref[0:1, :] == wanted
    second = routes_ref[1:2, :] == wanted
    named = jnp.where(first, 1.0, jnp.where(second, 1.0, 0.0))
    value = jnp.where(first, gates_ref[0:1, :], jnp.where(second, gates_ref[1:2, :], 0.0))
    earlier = jnp.where(
        lax.broadcasted_iota(jnp.int32, (count, count), 0) < lax.broadcasted_iota(jnp.int32, (count, count), 1),
        1.0, 0.0,
    ).astype(BF16)
    rank = dot(named.astype(BF16), earlier, 1, 0).astype(jnp.int32)
    place = jnp.where(named > 0.5, rank, -1)
    row_id = lax.broadcasted_iota(jnp.int32, (CAP, count), 0)
    scales = []
    for j in range(SLOTS):
        taken = place[j : j + 1, :] == row_id
        pack[pl.ds(j * CAP, CAP), :] = jnp.where(taken, 1.0, 0.0).astype(BF16)
        scales.append(jnp.sum(jnp.where(taken, value[j : j + 1, :], 0.0), axis=1, keepdims=True))

    def packed(lo, hi, tok, grad):
        chosen = pack[pl.ds(lo * CAP, (hi - lo) * CAP), :]
        taken_rows = dot(chosen, tok[...], 1, 0).astype(BF16)
        taken_grads = dot(chosen, grad[...], 1, 0)
        for j in range(lo, hi):
            part = slice((j - lo) * CAP, (j - lo + 1) * CAP)
            yield j, taken_rows[part], (taken_grads[part] * scales[j]).astype(BF16)

    def y_send(j):
        if j in NEAR:
            send(sendf.at[j - FAR], rows.at[j], y_s.at[j], y_r.at[j], at_y(SHIFTS[j]))
        else:
            send(sendq.at[j - 1], rows.at[j, :, quarter(0)], y_s.at[j], y_r.at[j], at_y(SHIFTS[j]))

    def y_arrived(j):
        part = rows.at[j] if j in NEAR else rows.at[j, :, quarter(0)]
        arrived(part, y_s.at[j], y_r.at[j], at_y(8 - SHIFTS[j]))

    def x_send(j):
        part = rows.at[j, :, quarter(0)]
        send(part, part, x_s.at[j - 1, 0], x_r.at[j - 1, 0], x_right)
        send(part, part, x_s.at[j - 1, 1], x_r.at[j - 1, 1], x_left)

    def x_forward(j):
        arrived(rows.at[j, :, quarter(3)], x_s.at[j - 1, 0], x_r.at[j - 1, 0], x_left)
        part = rows.at[j, pl.ds(0, CAP), quarter(3)]
        send(part, part, x_s.at[j - 1, 2], x_r.at[j - 1, 2], x_right)
        arrived(rows.at[j, :, quarter(1)], x_s.at[j - 1, 1], x_r.at[j - 1, 1], x_right)
        part = rows.at[j, pl.ds(CAP, CAP), quarter(1)]
        send(part, part, x_s.at[j - 1, 3], x_r.at[j - 1, 3], x_left)

    def x_complete(j):
        arrived(rows.at[j, pl.ds(0, CAP), quarter(2)], x_s.at[j - 1, 2], x_r.at[j - 1, 2], x_left)
        arrived(rows.at[j, pl.ds(CAP, CAP), quarter(2)], x_s.at[j - 1, 3], x_r.at[j - 1, 3], x_right)

    def weight_part(shift, core, half):
        if half is None:
            return weights.at[:, block(shift, core)]
        return weights.at[pl.ds(*HALVES[half]), block(shift, core)]

    def ag_shift(step, side):
        return (8 - step) % 8 if side == 0 else step

    def ag_halves(step, side):
        return (side,) if step == 4 else (0, 1)

    def ag_send(step, side, half):
        part = weight_part(ag_shift(step - 1, side), c, half)
        device = z_right if side == 0 else z_left
        send(part, part, ag_s.at[side, step - 1, half], ag_r.at[side, step - 1, half], device)

    def sib_half(step, side):
        return side if step == 4 else None

    def sib_send(step, side):
        index = 1 + 2 * (step - 1) + side if step else 0
        part = weight_part(ag_shift(step, side), c, sib_half(step, side))
        send(part, part, sg_s.at[index], sg_r.at[index], sibling)

    def ag_start():
        for half in (0, 1):
            for side in (0, 1):
                ag_send(1, side, half)
        sib_send(0, 0)

    def ag_step(step):
        for half in (0, 1):
            for side in (0, 1):
                if half in ag_halves(step, side):
                    arrived(
                        weight_part(ag_shift(step, side), c, half), ag_s.at[side, step - 1, half],
                        ag_r.at[side, step - 1, half], z_left if side == 0 else z_right,
                    )
                    if step < 4 and half in ag_halves(step + 1, side):
                        ag_send(step + 1, side, half)
        for side in (0, 1):
            sib_send(step, side)

    def weights_complete():
        arrived(weight_part(0, 1 - c, None), sg_s.at[0], sg_r.at[0], sibling)
        for step in range(1, 5):
            for side in (0, 1):
                index = 1 + 2 * (step - 1) + side
                part = weight_part(ag_shift(step, side), 1 - c, sib_half(step, side))
                arrived(part, sg_s.at[index], sg_r.at[index], sibling)

    backs, hids = (back_a, back_b), (hid_a, hid_b)

    def batch(b, lo, lanes=slice(None)):
        first, last = BATCHES[b]
        part = rows[first:last, lo : lo + CAP, lanes]
        return part.reshape((last - first) * CAP, part.shape[2])

    def forward(b):
        pre = dot(weights[0 : 2 * HID, :], batch(b, 0), 1, 1)
        back_hidden = dot(weights[2 * HID : HID3, :], batch(b, CAP), 1, 1)
        pre_gate, pre_up = pre[0:HID], pre[HID : 2 * HID]
        s = jax.nn.sigmoid(pre_gate)
        active = pre_gate * s
        hids[b][...] = (active * pre_up).astype(BF16)
        backs[b][0:HID, :] = (back_hidden * pre_up * s * (1.0 + pre_gate * (1.0 - s))).astype(BF16)
        backs[b][HID : 2 * HID, :] = (back_hidden * active).astype(BF16)

    def row_grads(b):
        first, last = BATCHES[b]
        for q in range(4):
            lanes = slice(q * width, (q + 1) * width)
            part = dot(backs[b][...], weights[0 : 2 * HID, lanes], 0, 0).astype(BF16)
            row_grad[first:last, :, lanes] = part.reshape(last - first, CAP, width)

    def rs_send(j):
        for index, (shift, device) in enumerate(((1, x_right), (3, x_left), (2, x_far))):
            send(
                row_grad.at[j, :, quarter(shift)], xs_in.at[j, index], xs_s.at[j, index], xs_r.at[j, index], device,
            )

    def rs_finish(j):
        total = row_grad[j, :, quarter(0)].astype(F32)
        for index, device in enumerate((x_left, x_right, x_far)):
            arrived(xs_in.at[j, index], xs_s.at[j, index], xs_r.at[j, index], device)
            total = total + xs_in[j, index].astype(F32)
        if j == 0:
            ret[0] = total.astype(BF16)
        else:
            yback[j] = total.astype(BF16)
            send(yback.at[j], ret.at[j], yb_s.at[j], yb_r.at[j], at_y(8 - SHIFTS[j]))

    def weight_early():
        for k in range(8):
            lanes = slice(256 * k, 256 * (k + 1))
            wacc[0 : 2 * HID, lanes] = dot(back_a[...], batch(0, 0, lanes), 1, 0)
            wacc[2 * HID : HID3, lanes] = dot(hid_a[...], batch(0, CAP, lanes), 1, 0)

    def weight_chunk(index, shift):
        lanes = pl.ds(pl.multiple_of(((z + shift) % 8) * 256, 256), 256)
        grad_gu = wacc[0 : 2 * HID, lanes] + dot(back_b[...], batch(1, 0, lanes), 1, 0)
        grad_d = wacc[2 * HID : HID3, lanes] + dot(hid_b[...], batch(1, CAP, lanes), 1, 0)
        wgrad[0 : 2 * HID, lanes] = grad_gu.astype(BF16)
        wgrad[2 * HID : HID3, lanes] = grad_d.astype(BF16)
        send(wgrad.at[:, block(shift, 1 - c)], sib_rs.at[index], sr_s.at[index], sr_r.at[index], sibling)

    chunk_shifts = (4, 3, 5, 2, 6, 1, 7, 0)

    def pair_ready(index):
        arrived(sib_rs.at[index], sr_s.at[index], sr_r.at[index], sibling)

    def pair_sum(index, lo, size):
        mine = wgrad[pl.ds(lo, size), block(chunk_shifts[index], c)].astype(F32)
        return mine + sib_rs[index, pl.ds(lo, size), :].astype(F32)

    def ring_part(ref, side, step, piece):
        return ref.at[side, step - 1, pl.ds(*PIECES[piece])]

    def ring_send(step, side, piece, total):
        lo, size = PIECES[piece]
        ring_out[side, step - 1, pl.ds(lo, size), :] = total.astype(BF16)
        send(
            ring_part(ring_out, side, step, piece), ring_part(ring_in, side, step, piece),
            rr_s.at[side, step - 1, piece], rr_r.at[side, step - 1, piece], z_right if side == 0 else z_left,
        )

    def ring_recv(step, side, piece):
        lo, size = PIECES[piece]
        arrived(
            ring_part(ring_in, side, step, piece), rr_s.at[side, step - 1, piece], rr_r.at[side, step - 1, piece],
            z_left if side == 0 else z_right,
        )
        return ring_in[side, step - 1, pl.ds(lo, size), :].astype(F32)

    def ring_step(step):
        if step == 1:
            pair_ready(0)
            for turn in (0, 1):
                for side in (0, 1):
                    piece = 2 * side + turn
                    ring_send(1, side, piece, pair_sum(0, *PIECES[piece]))
            return
        for side in (0, 1):
            pair_ready(2 * step - 3 + side)
        for turn in range(4):
            for side in (0, 1):
                piece = (turn + 2 * side) % 4
                total = pair_sum(2 * step - 3 + side, *PIECES[piece])
                if step > 2 or piece // 2 == side:
                    total = total + ring_recv(step - 1, side, piece)
                ring_send(step, side, piece, total)

    loads[2].wait()
    loads[3].wait()
    for j, part, grad_part in packed(1, FAR, tokq, gradq):
        sendq[j - 1, 0:CAP, :] = part
        sendq[j - 1, CAP : 2 * CAP, :] = grad_part
    pl.semaphore_wait(barrier, len(partners))

    for j in (1, 2, 3, 4):
        y_send(j)
    for copy in loads[4:7]:
        copy.wait()
    ag_start()
    loads[7].wait()
    loads[8].wait()
    for j, part, grad_part in packed(0, 1, tokf, gradf):
        rows[0, 0:CAP, :] = part
        rows[0, CAP : 2 * CAP, :] = grad_part
    for j, part, grad_part in packed(FAR, SLOTS, tokf, gradf):
        sendf[j - FAR, 0:CAP, :] = part
        sendf[j - FAR, CAP : 2 * CAP, :] = grad_part

    ag_step(1)
    for j in (1, 2):
        y_arrived(j)
        x_send(j)
    y_send(5)
    ag_step(2)
    x_forward(1)
    x_forward(2)
    for j in (3, 4):
        y_arrived(j)
        x_send(j)
    for j in NEAR:
        y_send(j)
    ag_step(3)
    y_arrived(5)
    x_send(5)
    x_complete(1)
    x_complete(2)
    ag_step(4)
    x_forward(3)
    x_forward(4)
    weights_complete()
    forward(0)
    x_forward(5)
    row_grads(0)
    for j in range(*BATCHES[0]):
        rs_send(j)
    weight_early()
    for j in (3, 4, 5):
        x_complete(j)
    for j in NEAR:
        y_arrived(j)

    forward(1)
    row_grads(1)
    for j in (5, 3, 4, 6, 7):
        rs_send(j)
    for index, shift in enumerate(chunk_shifts):
        weight_chunk(index, shift)
        if index == 1:
            ring_step(1)
    for j in (1, 2, 0):
        rs_finish(j)
    ring_step(2)
    rs_finish(5)
    rs_finish(3)
    ring_step(3)
    rs_finish(4)
    rs_finish(6)
    ring_step(4)
    rs_finish(7)

    pair_ready(7)
    outs = ((0, HID, gate_out), (HID, 2 * HID, up_out), (2 * HID, HID3, down_out))
    for piece in range(4):
        lo, size = PIECES[piece]
        total = pair_sum(7, lo, size) + ring_recv(4, 0, piece) + ring_recv(4, 1, piece)
        for first, last, out in outs:
            start, stop = max(first, lo), min(last, lo + size)
            if start < stop:
                out[0, start - first : stop - first] = total[start - lo : stop - lo]

    for j in range(1, SLOTS):
        arrived(ret.at[j], yb_s.at[j], yb_r.at[j], at_y(SHIFTS[j]))
    back_rows = ret[...].reshape(SLOTS * CAP, width)
    tok_out[...] = dot(pack[...], back_rows, 0, 0).astype(BF16)

    for copy in pending:
        copy.wait_send()


def on_device(tokens, out_grad, routes, gate_values, gate_proj, up_proj, down_proj):
    count, model = tokens.shape
    width = model // lax.axis_size("mp")
    sems = pltpu.SemaphoreType.DMA
    vmem = pl.BlockSpec(memory_space=pltpu.VMEM)
    hbm = pl.BlockSpec(memory_space=pltpu.HBM)
    weight_out = jax.ShapeDtypeStruct(gate_proj.shape, F32)
    return pl.pallas_call(
        kernel,
        out_shape=(jax.ShapeDtypeStruct((count, width), BF16), weight_out, weight_out, weight_out),
        in_specs=[hbm] * 7,
        out_specs=(vmem, vmem, vmem, vmem),
        scratch_shapes=[
            pltpu.VMEM((count, width), BF16),
            pltpu.VMEM((count, width), BF16),
            pltpu.VMEM((count, model), BF16),
            pltpu.VMEM((count, model), BF16),
            pltpu.VMEM((2, count), jnp.int32),
            pltpu.VMEM((2, count), F32),
            pltpu.VMEM((SLOTS * CAP, count), BF16),
            pltpu.VMEM((FAR - 1, 2 * CAP, width), BF16),
            pltpu.VMEM((len(NEAR), 2 * CAP, model), BF16),
            pltpu.VMEM((SLOTS, 2 * CAP, model), BF16),
            pltpu.VMEM((HID3, model), BF16),
            *(pltpu.VMEM((2 * HID, (last - first) * CAP), BF16) for first, last in BATCHES),
            *(pltpu.VMEM((HID, (last - first) * CAP), BF16) for first, last in BATCHES),
            pltpu.VMEM((SLOTS, CAP, model), BF16),
            pltpu.VMEM((HID3, model), F32),
            pltpu.VMEM((HID3, model), BF16),
            pltpu.VMEM((8, HID3, 128), BF16),
            pltpu.VMEM((2, 4, HID3, 128), BF16),
            pltpu.VMEM((2, 4, HID3, 128), BF16),
            pltpu.VMEM((SLOTS, 3, CAP, width), BF16),
            pltpu.VMEM((SLOTS, CAP, width), BF16),
            pltpu.VMEM((SLOTS, CAP, width), BF16),
            sems((9,)),
            sems((SLOTS,)),
            sems((SLOTS,)),
            sems((FAR - 1, 4)),
            sems((FAR - 1, 4)),
            sems((2, 4, 2)),
            sems((2, 4, 2)),
            sems((9,)),
            sems((9,)),
            sems((SLOTS, 3)),
            sems((SLOTS, 3)),
            sems((SLOTS,)),
            sems((SLOTS,)),
            sems((8,)),
            sems((8,)),
            sems((2, 4, 4)),
            sems((2, 4, 4)),
        ],
        compiler_params=pltpu.CompilerParams(
            collective_id=0, has_side_effects=True, vmem_limit_bytes=56 * 1024 * 1024
        ),
        cost_estimate=pl.CostEstimate(flops=2300000000, bytes_accessed=4000000, transcendentals=70000),
        name="experts",
    )(tokens, out_grad, routes.T, gate_values.T, gate_proj, up_proj, down_proj)


def solution(mesh):
    tokens_in = P(("dp", "expert"), None)
    weights_in = P("expert", "mp", "dp")
    return jax.shard_map(
        on_device,
        mesh=mesh,
        in_specs=(tokens_in, tokens_in, tokens_in, tokens_in, weights_in, weights_in, weights_in),
        out_specs=(P(("dp", "expert"), "mp"), weights_in, weights_in, weights_in),
        check_vma=False,
    )
```

time: 82.7 us -> 70.3 us (0.85)
  Pallas kernels: 73.8 us -> 65.3 us
  local copies, waits for them, and re-layouts: 7.7 us -> 4.09 us
    pallas_call x1, Pallas kernels: 73.8 us -> 65.3 us  [on_device(): pl.pallas_call(kernel, out_shape=(jax.ShapeDtypeStruct((count, width), BF...]
    unnamed x18 -> x10, local copies, waits for them, and re-layouts: 7.7 us -> 4.09 us
where the time goes in v2:
time: 70.3 us; the launch traced here: 70 us
  Pallas kernels  65.3 us (93%)
  local copies, waits for them, and re-layouts  4.09 us (6%)
    pallas_call x1, Pallas kernels, on_device(): pl.pallas_call(kernel, out_shape=(jax.ShapeDtypeStruct((count, width), BF...  65.3 us
    unnamed x10, local copies, waits for them, and re-layouts  4.09 us

profile of v2, /device:TPU:1, one launch (start us, length us, event | category | flops | bytes accessed | tf_op | source)
XLA Modules:
  0.0 70.0 jit_solution(511259408878309052)
XLA Ops:
  0.6 65.3 %experts.1 = (bf16[128,512]{1,0:T(8,128)(2,1)}, f32[1,176,128]{2,1,0:T(8,128)}, f32[1,176,128]{2,1,0:T(8,128)}, f32[1,176,128]{2,1,0:T(8,128)}) custom-call(bf16[128,2048]{1,0:T(8,128)(2,1)} %tok_hbm.1, bf16[128,2048]{1,0:T(8,128)(2,1)} %grad_hbm.1, s32[2,128]{1,0:T(2,128)} %bitcast.2, f32[2,128]{1,0:T(2,128)} %bitcast.3, bf16[1,176,128]{2,1,0:T(8,128)(2,1)} %gate_hbm.1, ...), custom_call_target="tpu_custom_call" | custom-call | flops 2300000000 | bytes 4000000 | tf_op jit(solution)/shard_map/experts/pallas_call | solution.py:404
  65.9 0.0 copy-start.2
  65.9 1.6 %copy.15 = bf16[128,512]{1,0:T(8,128)(2,1)} copy(bf16[128,512]{1,0:T(8,128)(2,1)} %get-tuple-element.8) | data formatting | bytes 262144
  67.5 0.0 copy-done.2
  67.5 0.0 copy-start.1
  67.5 0.6 copy.16
  68.2 0.3 copy-done.1
  68.5 0.0 copy-start
  68.5 0.6 copy.17
  69.1 0.3 copy-done
  69.4 0.6 copy.18
Async XLA Ops:
  65.9 1.6 %copy-start.2 = (f32[1,176,128]{2,1,0:T(8,128)S(1)}, f32[1,176,128]{2,1,0:T(8,128)}, u32[]{:S(2)}) copy-start(f32[1,176,128]{2,1,0:T(8,128)} %get-tuple-element.9) | copy-start | bytes 270340
  67.5 0.9 %copy-start.1 = (f32[1,176,128]{2,1,0:T(8,128)S(1)}, f32[1,176,128]{2,1,0:T(8,128)}, u32[]{:S(2)}) copy-start(f32[1,176,128]{2,1,0:T(8,128)} %get-tuple-element.10) | copy-start | bytes 270340
  68.5 0.9 %copy-start = (f32[1,176,128]{2,1,0:T(8,128)S(1)}, f32[1,176,128]{2,1,0:T(8,128)}, u32[]{:S(2)}) copy-start(f32[1,176,128]{2,1,0:T(8,128)} %get-tuple-element.11) | copy-start | bytes 270340

commit v3 on v2

--- a/solution.py
+++ b/solution.py
@@ -15,7 +15,10 @@
 SLOTS = 8
 FAR = 6
 NEAR = (6, 7)
-BATCHES = ((0, 3), (3, 8))
+SPLIT = (1, 2, 3, 4)
+LAST_FAR = 5
+BATCHES = ((0, 3), (3, 5), (5, 6), (6, 8))
+GROUPS = ((1, 3),)
 CAP = 48
 HID = 176
 HID3 = 3 * HID
@@ -31,8 +34,8 @@
     tok_hbm, grad_hbm, routes_hbm, gates_hbm, gate_hbm, up_hbm, down_hbm,
     tok_out, gate_out, up_out, down_out,
     tokq, gradq, tokf, gradf, routes_ref, gates_ref, pack, sendq, sendf, rows, weights, back_a, back_b, hid_a, hid_b,
-    row_grad, wacc, wgrad, sib_rs, ring_in, ring_out, xs_in, yback, ret,
-    loc, y_s, y_r, x_s, x_r, ag_s, ag_r, sg_s, sg_r, xs_s, xs_r, yb_s, yb_r, sr_s, sr_r, rr_s, rr_r,
+    row_grad, wacc, wgrad, sib_rs, ring_in, ring_out, xs_in, gr_in, gx_in, yback, ret,
+    loc, y_s, y_r, x_s, x_r, ag_s, ag_r, sg_s, sg_r, xs_s, xs_r, gs_s, gs_r, yb_s, yb_r, sr_s, sr_r, rr_s, rr_r,
 ):
     d, e, m = lax.axis_index("dp"), lax.axis_index("expert"), lax.axis_index("mp")
     z, c = d // 2, d % 2
@@ -48,6 +51,7 @@
         return (d, e, (m + shift) % 4)
 
     z_right, z_left, sibling = at_z(1), at_z(7), at_z(0, 1 - c)
+    z_right2, z_left2 = at_z(2), at_z(6)
     x_right, x_left, x_far = at_x(1), at_x(3), at_x(2)
 
     def quarter(shift):
@@ -72,7 +76,7 @@
         remote(dst, dst, send_sem, recv_sem, device).wait_recv()
 
     barrier = pltpu.get_barrier_semaphore()
-    partners = [z_right, z_left, sibling, x_right, x_left, x_far] + [at_y(k) for k in range(1, 8)]
+    partners = [z_right, z_left, z_right2, z_left2, sibling, x_right, x_left, x_far] + [at_y(k) for k in range(1, 8)]
     for partner in partners:
         pl.semaphore_signal(barrier, inc=1, device_id=partner, device_id_type=MESH)
 
@@ -123,32 +127,53 @@
             part = slice((j - lo) * CAP, (j - lo + 1) * CAP)
             yield j, taken_rows[part], (taken_grads[part] * scales[j]).astype(BF16)
 
-    def y_send(j):
+    both, token_rows, grad_rows = pl.ds(0, 2 * CAP), pl.ds(0, CAP), pl.ds(CAP, CAP)
+
+    def y_send(j, part=0, span=both):
         if j in NEAR:
-            send(sendf.at[j - FAR], rows.at[j], y_s.at[j], y_r.at[j], at_y(SHIFTS[j]))
+            send(sendf.at[j - FAR], rows.at[j], y_s.at[j, 0], y_r.at[j, 0], at_y(SHIFTS[j]))
         else:
-            send(sendq.at[j - 1], rows.at[j, :, quarter(0)], y_s.at[j], y_r.at[j], at_y(SHIFTS[j]))
-
-    def y_arrived(j):
-        part = rows.at[j] if j in NEAR else rows.at[j, :, quarter(0)]
-        arrived(part, y_s.at[j], y_r.at[j], at_y(8 - SHIFTS[j]))
-
-    def x_send(j):
-        part = rows.at[j, :, quarter(0)]
-        send(part, part, x_s.at[j - 1, 0], x_r.at[j - 1, 0], x_right)
-        send(part, part, x_s.at[j - 1, 1], x_r.at[j - 1, 1], x_left)
-
-    def x_forward(j):
-        arrived(rows.at[j, :, quarter(3)], x_s.at[j - 1, 0], x_r.at[j - 1, 0], x_left)
-        part = rows.at[j, pl.ds(0, CAP), quarter(3)]
-        send(part, part, x_s.at[j - 1, 2], x_r.at[j - 1, 2], x_right)
-        arrived(rows.at[j, :, quarter(1)], x_s.at[j - 1, 1], x_r.at[j - 1, 1], x_right)
-        part = rows.at[j, pl.ds(CAP, CAP), quarter(1)]
-        send(part, part, x_s.at[j - 1, 3], x_r.at[j - 1, 3], x_left)
+            send(
+                sendq.at[j - 1, span], rows.at[j, span, quarter(0)], y_s.at[j, part], y_r.at[j, part], at_y(SHIFTS[j]),
+            )
+
+    def y_arrived(j, part=0, span=both):
+        where = rows.at[j] if j in NEAR else rows.at[j, span, quarter(0)]
+        arrived(where, y_s.at[j, part], y_r.at[j, part], at_y(8 - SHIFTS[j]))
+
+    def x_send(j, part=0, span=both):
+        block_out = rows.at[j, span, quarter(0)]
+        send(block_out, block_out, x_s.at[j - 1, part, 0], x_r.at[j - 1, part, 0], x_right)
+        send(block_out, block_out, x_s.at[j - 1, part, 1], x_r.at[j - 1, part, 1], x_left)
+        if j == LAST_FAR:
+            send(block_out, block_out, x_s.at[j - 1, part, 2], x_r.at[j - 1, part, 2], x_far)
+
+    def x_arrived(j, side, part=0, span=both):
+        shift, device = ((3, x_left), (1, x_right), (2, x_far))[side]
+        arrived(rows.at[j, span, quarter(shift)], x_s.at[j - 1, part, side], x_r.at[j - 1, part, side], device)
+
+    def forward_send(j, side):
+        block_out = rows.at[j, grad_rows if side else token_rows, quarter(1 if side else 3)]
+        device = x_left if side else x_right
+        send(block_out, block_out, x_s.at[j - 1, side, 2], x_r.at[j - 1, side, 2], device)
+
+    def x_forward(j, side):
+        if j in SPLIT:
+            x_arrived(j, side, side, (token_rows, grad_rows)[side])
+        else:
+            x_arrived(j, side)
+        forward_send(j, side)
 
     def x_complete(j):
-        arrived(rows.at[j, pl.ds(0, CAP), quarter(2)], x_s.at[j - 1, 2], x_r.at[j - 1, 2], x_left)
-        arrived(rows.at[j, pl.ds(CAP, CAP), quarter(2)], x_s.at[j - 1, 3], x_r.at[j - 1, 3], x_right)
+        if j == LAST_FAR:
+            for side in (0, 1, 2):
+                x_arrived(j, side)
+            return
+        if j in SPLIT:
+            x_arrived(j, 1, 0, token_rows)
+            x_arrived(j, 0, 1, grad_rows)
+        arrived(rows.at[j, token_rows, quarter(2)], x_s.at[j - 1, 0, 2], x_r.at[j - 1, 0, 2], x_left)
+        arrived(rows.at[j, grad_rows, quarter(2)], x_s.at[j - 1, 1, 2], x_r.at[j - 1, 1, 2], x_right)
 
     def weight_part(shift, core, half):
         if half is None:
@@ -175,6 +200,8 @@
         send(part, part, sg_s.at[index], sg_r.at[index], sibling)
 
     def ag_start():
+        for copy in loads[4:7]:
+            copy.wait()
         for half in (0, 1):
             for side in (0, 1):
                 ag_send(1, side, half)
@@ -201,28 +228,35 @@
                 part = weight_part(ag_shift(step, side), 1 - c, sib_half(step, side))
                 arrived(part, sg_s.at[index], sg_r.at[index], sibling)
 
-    backs, hids = (back_a, back_b), (hid_a, hid_b)
-
-    def batch(b, lo, lanes=slice(None)):
+    def hidden_terms(b):
         first, last = BATCHES[b]
+        base = 0 if b == 0 else BATCHES[1][0]
+        lanes = slice((first - base) * CAP, (last - base) * CAP)
+        return (back_a, hid_a, lanes) if b == 0 else (back_b, hid_b, lanes)
+
+
+    def batch(first, last, lo, lanes=slice(None)):
         part = rows[first:last, lo : lo + CAP, lanes]
         return part.reshape((last - first) * CAP, part.shape[2])
 
     def forward(b):
-        pre = dot(weights[0 : 2 * HID, :], batch(b, 0), 1, 1)
-        back_hidden = dot(weights[2 * HID : HID3, :], batch(b, CAP), 1, 1)
+        first, last = BATCHES[b]
+        pre = dot(weights[0 : 2 * HID, :], batch(first, last, 0), 1, 1)
+        back_hidden = dot(weights[2 * HID : HID3, :], batch(first, last, CAP), 1, 1)
         pre_gate, pre_up = pre[0:HID], pre[HID : 2 * HID]
         s = jax.nn.sigmoid(pre_gate)
         active = pre_gate * s
-        hids[b][...] = (active * pre_up).astype(BF16)
-        backs[b][0:HID, :] = (back_hidden * pre_up * s * (1.0 + pre_gate * (1.0 - s))).astype(BF16)
-        backs[b][HID : 2 * HID, :] = (back_hidden * active).astype(BF16)
+        back_ref, hid_ref, lanes = hidden_terms(b)
+        hid_ref[:, lanes] = (active * pre_up).astype(BF16)
+        back_ref[0:HID, lanes] = (back_hidden * pre_up * s * (1.0 + pre_gate * (1.0 - s))).astype(BF16)
+        back_ref[HID : 2 * HID, lanes] = (back_hidden * active).astype(BF16)
 
     def row_grads(b):
         first, last = BATCHES[b]
+        back_ref, _, terms = hidden_terms(b)
         for q in range(4):
             lanes = slice(q * width, (q + 1) * width)
-            part = dot(backs[b][...], weights[0 : 2 * HID, lanes], 0, 0).astype(BF16)
+            part = dot(back_ref[:, terms], weights[0 : 2 * HID, lanes], 0, 0).astype(BF16)
             row_grad[first:last, :, lanes] = part.reshape(last - first, CAP, width)
 
     def rs_send(j):
@@ -242,16 +276,52 @@
             yback[j] = total.astype(BF16)
             send(yback.at[j], ret.at[j], yb_s.at[j], yb_r.at[j], at_y(8 - SHIFTS[j]))
 
+    def half_quarter(shift, side):
+        return pl.ds(pl.multiple_of(((m + shift) % 4) * width + side * (width // 2), width // 2), width // 2)
+
+    def group_start(g):
+        first, last = GROUPS[g]
+        for side, device in enumerate((x_right, x_left)):
+            send(
+                row_grad.at[first:last, :, half_quarter(2, side)], gr_in.at[side, first:last],
+                gs_s.at[g, side], gs_r.at[g, side], device,
+            )
+
+    def group_pass(g):
+        first, last = GROUPS[g]
+        for side, (shift, device, source) in enumerate(((1, x_right, x_left), (3, x_left, x_right))):
+            arrived(gr_in.at[side, first:last], gs_s.at[g, side], gs_r.at[g, side], source)
+            lanes = half_quarter(shift, side)
+            for j in range(first, last):
+                total = row_grad[j, :, lanes].astype(F32) + gr_in[side, j].astype(F32)
+                row_grad[j, :, lanes] = total.astype(BF16)
+            send(
+                row_grad.at[first:last, :, quarter(shift)], gx_in.at[side, first:last],
+                gs_s.at[g, 2 + side], gs_r.at[g, 2 + side], device,
+            )
+
+    def group_finish(g):
+        first, last = GROUPS[g]
+        for side, source in enumerate((x_left, x_right)):
+            arrived(gx_in.at[side, first:last], gs_s.at[g, 2 + side], gs_r.at[g, 2 + side], source)
+        for j in range(first, last):
+            total = row_grad[j, :, quarter(0)].astype(F32) + gx_in[0, j].astype(F32) + gx_in[1, j].astype(F32)
+            yback[j] = total.astype(BF16)
+            send(yback.at[j], ret.at[j], yb_s.at[j], yb_r.at[j], at_y(8 - SHIFTS[j]))
+
     def weight_early():
+        first, last = BATCHES[0]
         for k in range(8):
             lanes = slice(256 * k, 256 * (k + 1))
-            wacc[0 : 2 * HID, lanes] = dot(back_a[...], batch(0, 0, lanes), 1, 0)
-            wacc[2 * HID : HID3, lanes] = dot(hid_a[...], batch(0, CAP, lanes), 1, 0)
-
-    def weight_chunk(index, shift):
+            wacc[0 : 2 * HID, lanes] = dot(back_a[...], batch(first, last, 0, lanes), 1, 0)
+            wacc[2 * HID : HID3, lanes] = dot(hid_a[...], batch(first, last, CAP, lanes), 1, 0)
+
+    def weight_chunk(index):
+        shift = chunk_shifts[index]
+        first, last = BATCHES[1][0], SLOTS
         lanes = pl.ds(pl.multiple_of(((z + shift) % 8) * 256, 256), 256)
-        grad_gu = wacc[0 : 2 * HID, lanes] + dot(back_b[...], batch(1, 0, lanes), 1, 0)
-        grad_d = wacc[2 * HID : HID3, lanes] + dot(hid_b[...], batch(1, CAP, lanes), 1, 0)
+        grad_gu = wacc[0 : 2 * HID, lanes] + dot(back_b[...], batch(first, last, 0, lanes), 1, 0)
+        grad_d = wacc[2 * HID : HID3, lanes] + dot(hid_b[...], batch(first, last, CAP, lanes), 1, 0)
         wgrad[0 : 2 * HID, lanes] = grad_gu.astype(BF16)
         wgrad[2 * HID : HID3, lanes] = grad_d.astype(BF16)
         send(wgrad.at[:, block(shift, 1 - c)], sib_rs.at[index], sr_s.at[index], sr_r.at[index], sibling)
@@ -265,143 +335,204 @@
         mine = wgrad[pl.ds(lo, size), block(chunk_shifts[index], c)].astype(F32)
         return mine + sib_rs[index, pl.ds(lo, size), :].astype(F32)
 
-    def ring_part(ref, side, step, piece):
-        return ref.at[side, step - 1, pl.ds(*PIECES[piece])]
-
-    def ring_send(step, side, piece, total):
+    def ring_part(ref, side, slot, piece):
+        return ref.at[side, slot, pl.ds(*PIECES[piece])]
+
+    def ring_send(side, slot, piece, total):
         lo, size = PIECES[piece]
-        ring_out[side, step - 1, pl.ds(lo, size), :] = total.astype(BF16)
+        ring_out[side, slot, pl.ds(lo, size), :] = total.astype(BF16)
         send(
-            ring_part(ring_out, side, step, piece), ring_part(ring_in, side, step, piece),
-            rr_s.at[side, step - 1, piece], rr_r.at[side, step - 1, piece], z_right if side == 0 else z_left,
+            ring_part(ring_out, side, slot, piece), ring_part(ring_in, side, slot, piece),
+            rr_s.at[side, slot, piece], rr_r.at[side, slot, piece],
+            ((z_right, z_left), (z_right2, z_left2))[slot == 0][side],
         )
 
-    def ring_recv(step, side, piece):
+    def ring_recv(side, slot, piece):
         lo, size = PIECES[piece]
         arrived(
-            ring_part(ring_in, side, step, piece), rr_s.at[side, step - 1, piece], rr_r.at[side, step - 1, piece],
-            z_left if side == 0 else z_right,
+            ring_part(ring_in, side, slot, piece), rr_s.at[side, slot, piece], rr_r.at[side, slot, piece],
+            ((z_left, z_right), (z_left2, z_right2))[slot == 0][side],
         )
-        return ring_in[side, step - 1, pl.ds(lo, size), :].astype(F32)
-
-    def ring_step(step):
-        if step == 1:
-            pair_ready(0)
-            for turn in (0, 1):
-                for side in (0, 1):
-                    piece = 2 * side + turn
-                    ring_send(1, side, piece, pair_sum(0, *PIECES[piece]))
-            return
-        for side in (0, 1):
-            pair_ready(2 * step - 3 + side)
+        return ring_in[side, slot, pl.ds(lo, size), :].astype(F32)
+
+    def ring_order():
         for turn in range(4):
             for side in (0, 1):
-                piece = (turn + 2 * side) % 4
-                total = pair_sum(2 * step - 3 + side, *PIECES[piece])
-                if step > 2 or piece // 2 == side:
-                    total = total + ring_recv(step - 1, side, piece)
-                ring_send(step, side, piece, total)
+                yield side, (turn + 2 * (1 - side)) % 4
+
+    def ring_far():
+        pair_ready(0)
+        for turn in (0, 1):
+            for side in (0, 1):
+                piece = 2 * side + turn
+                ring_send(side, 0, piece, pair_sum(0, *PIECES[piece]))
+
+    def ring_first():
+        for side in (0, 1):
+            pair_ready(1 + side)
+        for side, piece in ring_order():
+            ring_send(side, 1, piece, pair_sum(1 + side, *PIECES[piece]))
+
+    def ring_step(slot, half):
+        if half == 0:
+            for side in (0, 1):
+                pair_ready(2 * slot - 1 + side)
+        for side, piece in tuple(ring_order())[4 * half : 4 * half + 4]:
+            total = pair_sum(2 * slot - 1 + side, *PIECES[piece]) + ring_recv(side, slot - 1, piece)
+            if slot == 2 and piece // 2 == side:
+                total = total + ring_recv(side, 0, piece)
+            ring_send(side, slot, piece, total)
+
+    def weight_outputs():
+        pair_ready(7)
+        outs = ((0, HID, gate_out), (HID, 2 * HID, up_out), (2 * HID, HID3, down_out))
+        for piece in range(4):
+            lo, size = PIECES[piece]
+            total = pair_sum(7, lo, size) + ring_recv(0, 3, piece) + ring_recv(1, 3, piece)
+            for first, last, out in outs:
+                start, stop = max(first, lo), min(last, lo + size)
+                if start < stop:
+                    out[0, start - first : stop - first] = total[start - lo : stop - lo]
+
+    def token_outputs():
+        for j in range(1, SLOTS):
+            arrived(ret.at[j], yb_s.at[j], yb_r.at[j], at_y(SHIFTS[j]))
+        back_rows = ret[...].reshape(SLOTS * CAP, width)
+        tok_out[...] = dot(pack[...], back_rows, 0, 0).astype(BF16)
+
+    def pack_full():
+        loads[7].wait()
+        loads[8].wait()
+        for j, part, grad_part in packed(0, 1, tokf, gradf):
+            rows[0, 0:CAP, :] = part
+            rows[0, CAP : 2 * CAP, :] = grad_part
+        for j, part, grad_part in packed(FAR, SLOTS, tokf, gradf):
+            sendf[j - FAR, 0:CAP, :] = part
+            sendf[j - FAR, CAP : 2 * CAP, :] = grad_part
+
+    def pack_quarter(lo, hi):
+        for j, part, grad_part in packed(lo, hi, tokq, gradq):
+            sendq[j - 1, 0:CAP, :] = part
+            sendq[j - 1, CAP : 2 * CAP, :] = grad_part
 
     loads[2].wait()
     loads[3].wait()
-    for j, part, grad_part in packed(1, FAR, tokq, gradq):
-        sendq[j - 1, 0:CAP, :] = part
-        sendq[j - 1, CAP : 2 * CAP, :] = grad_part
+    pack_quarter(1, 3)
     pl.semaphore_wait(barrier, len(partners))
 
-    for j in (1, 2, 3, 4):
-        y_send(j)
-    for copy in loads[4:7]:
-        copy.wait()
+    y_send(1, 1, grad_rows)
+    y_send(2, 0, token_rows)
+    y_send(1, 0, token_rows)
     ag_start()
-    loads[7].wait()
-    loads[8].wait()
-    for j, part, grad_part in packed(0, 1, tokf, gradf):
-        rows[0, 0:CAP, :] = part
-        rows[0, CAP : 2 * CAP, :] = grad_part
-    for j, part, grad_part in packed(FAR, SLOTS, tokf, gradf):
-        sendf[j - FAR, 0:CAP, :] = part
-        sendf[j - FAR, CAP : 2 * CAP, :] = grad_part
-
+    pack_quarter(3, FAR)
+    pack_full()
+    y_send(2, 1, grad_rows)
+    y_send(4, 1, grad_rows)
+    y_send(4, 0, token_rows)
+    y_send(3, 0, token_rows)
+    y_arrived(2, 0, token_rows)
+    x_send(2, 0, token_rows)
     ag_step(1)
-    for j in (1, 2):
-        y_arrived(j)
-        x_send(j)
+    y_send(3, 1, grad_rows)
     y_send(5)
+    y_arrived(1, 1, grad_rows)
+    x_send(1, 1, grad_rows)
+    y_arrived(1, 0, token_rows)
+    x_send(1, 0, token_rows)
+    y_send(7)
+    y_arrived(2, 1, grad_rows)
+    x_send(2, 1, grad_rows)
+    y_arrived(3, 0, token_rows)
+    x_send(3, 0, token_rows)
+    y_arrived(4, 1, grad_rows)
+    x_send(4, 1, grad_rows)
     ag_step(2)
-    x_forward(1)
-    x_forward(2)
-    for j in (3, 4):
-        y_arrived(j)
-        x_send(j)
-    for j in NEAR:
-        y_send(j)
+    x_forward(2, 1)
+    x_forward(1, 0)
+    y_send(6)
+    y_arrived(3, 1, grad_rows)
+    x_send(3, 1, grad_rows)
+    y_arrived(4, 0, token_rows)
+    x_send(4, 0, token_rows)
+    x_forward(4, 1)
+    x_forward(2, 0)
     ag_step(3)
+    x_forward(3, 0)
+    x_forward(1, 1)
+    x_forward(3, 1)
+    x_forward(4, 0)
     y_arrived(5)
     x_send(5)
     x_complete(1)
     x_complete(2)
     ag_step(4)
-    x_forward(3)
-    x_forward(4)
     weights_complete()
+    x_complete(3)
     forward(0)
-    x_forward(5)
+    x_complete(4)
     row_grads(0)
-    for j in range(*BATCHES[0]):
-        rs_send(j)
-    weight_early()
-    for j in (3, 4, 5):
-        x_complete(j)
-    for j in NEAR:
-        y_arrived(j)
-
+    group_start(0)
     forward(1)
     row_grads(1)
-    for j in (5, 3, 4, 6, 7):
-        rs_send(j)
-    for index, shift in enumerate(chunk_shifts):
-        weight_chunk(index, shift)
-        if index == 1:
-            ring_step(1)
-    for j in (1, 2, 0):
-        rs_finish(j)
-    ring_step(2)
+    rs_send(3)
+    weight_early()
+    y_arrived(7)
+    y_arrived(6)
+    forward(3)
+    rs_send(4)
+    x_complete(5)
+    forward(2)
+    weight_chunk(0)
+    row_grads(2)
+    group_pass(0)
+    weight_chunk(1)
+    weight_chunk(2)
+    ring_far()
+    rs_send(5)
+    ring_first()
+    row_grads(3)
+    rs_finish(3)
+    weight_chunk(3)
+    rs_send(7)
+    rs_send(6)
+    rs_finish(4)
+    rs_send(0)
+    weight_chunk(4)
+    weight_chunk(5)
+    group_finish(0)
+    weight_chunk(6)
+    weight_chunk(7)
+    ring_step(2, 0)
+    ring_step(2, 1)
     rs_finish(5)
-    rs_finish(3)
-    ring_step(3)
-    rs_finish(4)
+    ring_step(3, 0)
+    rs_finish(7)
+    ring_step(3, 1)
     rs_finish(6)
-    ring_step(4)
-    rs_finish(7)
-
-    pair_ready(7)
-    outs = ((0, HID, gate_out), (HID, 2 * HID, up_out), (2 * HID, HID3, down_out))
-    for piece in range(4):
-        lo, size = PIECES[piece]
-        total = pair_sum(7, lo, size) + ring_recv(4, 0, piece) + ring_recv(4, 1, piece)
-        for first, last, out in outs:
-            start, stop = max(first, lo), min(last, lo + size)
-            if start < stop:
-                out[0, start - first : stop - first] = total[start - lo : stop - lo]
-
-    for j in range(1, SLOTS):
-        arrived(ret.at[j], yb_s.at[j], yb_r.at[j], at_y(SHIFTS[j]))
-    back_rows = ret[...].reshape(SLOTS * CAP, width)
-    tok_out[...] = dot(pack[...], back_rows, 0, 0).astype(BF16)
+    rs_finish(0)
+    weight_outputs()
+    token_outputs()
 
     for copy in pending:
         copy.wait_send()
+
+
+def finish(tok_ref, gate_ref, up_ref, down_ref, tok_out, gate_out, up_out, down_out):
+    tok_out[...] = tok_ref[...]
+    gate_out[...] = gate_ref[...]
+    up_out[...] = up_ref[...]
+    down_out[...] = down_ref[...]
 
 
 def on_device(tokens, out_grad, routes, gate_values, gate_proj, up_proj, down_proj):
     count, model = tokens.shape
     width = model // lax.axis_size("mp")
     sems = pltpu.SemaphoreType.DMA
+    early = BATCHES[0][1]
     vmem = pl.BlockSpec(memory_space=pltpu.VMEM)
     hbm = pl.BlockSpec(memory_space=pltpu.HBM)
     weight_out = jax.ShapeDtypeStruct(gate_proj.shape, F32)
-    return pl.pallas_call(
+    results = pl.pallas_call(
         kernel,
         out_shape=(jax.ShapeDtypeStruct((count, width), BF16), weight_out, weight_out, weight_out),
         in_specs=[hbm] * 7,
@@ -418,8 +549,10 @@
             pltpu.VMEM((len(NEAR), 2 * CAP, model), BF16),
             pltpu.VMEM((SLOTS, 2 * CAP, model), BF16),
             pltpu.VMEM((HID3, model), BF16),
-            *(pltpu.VMEM((2 * HID, (last - first) * CAP), BF16) for first, last in BATCHES),
-            *(pltpu.VMEM((HID, (last - first) * CAP), BF16) for first, last in BATCHES),
+            pltpu.VMEM((2 * HID, early * CAP), BF16),
+            pltpu.VMEM((2 * HID, (SLOTS - early) * CAP), BF16),
+            pltpu.VMEM((HID, early * CAP), BF16),
+            pltpu.VMEM((HID, (SLOTS - early) * CAP), BF16),
             pltpu.VMEM((SLOTS, CAP, model), BF16),
             pltpu.VMEM((HID3, model), F32),
             pltpu.VMEM((HID3, model), BF16),
@@ -427,19 +560,23 @@
             pltpu.VMEM((2, 4, HID3, 128), BF16),
             pltpu.VMEM((2, 4, HID3, 128), BF16),
             pltpu.VMEM((SLOTS, 3, CAP, width), BF16),
+            pltpu.VMEM((2, SLOTS, CAP, width // 2), BF16),
+            pltpu.VMEM((2, SLOTS, CAP, width), BF16),
             pltpu.VMEM((SLOTS, CAP, width), BF16),
             pltpu.VMEM((SLOTS, CAP, width), BF16),
             sems((9,)),
-            sems((SLOTS,)),
-            sems((SLOTS,)),
-            sems((FAR - 1, 4)),
-            sems((FAR - 1, 4)),
+            sems((FAR + len(NEAR), 2)),
+            sems((FAR + len(NEAR), 2)),
+            sems((FAR - 1, 2, 3)),
+            sems((FAR - 1, 2, 3)),
             sems((2, 4, 2)),
             sems((2, 4, 2)),
             sems((9,)),
             sems((9,)),
             sems((SLOTS, 3)),
             sems((SLOTS, 3)),
+            sems((len(GROUPS), 4)),
+            sems((len(GROUPS), 4)),
             sems((SLOTS,)),
             sems((SLOTS,)),
             sems((8,)),
@@ -453,6 +590,13 @@
         cost_estimate=pl.CostEstimate(flops=2300000000, bytes_accessed=4000000, transcendentals=70000),
         name="experts",
     )(tokens, out_grad, routes.T, gate_values.T, gate_proj, up_proj, down_proj)
+    return pl.pallas_call(
+        finish,
+        out_shape=tuple(jax.ShapeDtypeStruct(result.shape, result.dtype) for result in results),
+        in_specs=[vmem] * 4,
+        out_specs=(vmem,) * 4,
+        name="finish",
+    )(*results)
 
 
 def solution(mesh):

time: 70.3 us -> 67.1 us (0.954)
  local copies, waits for them, and re-layouts: 4.09 us -> 0 us
  Pallas kernels: 65.3 us -> 66.2 us
    unnamed x10 -> x0, local copies, waits for them, and re-layouts: 4.09 us -> none
    pallas_call x0 -> x1, Pallas kernels: none -> 1.79 us  [on_device(): pl.pallas_call(finish, out_shape=tuple((jax.ShapeDtypeStruct(result.shape...]
    pallas_call x1, Pallas kernels: 65.3 us -> 64.4 us  [on_device(): pl.pallas_call(kernel, out_shape=(jax.ShapeDtypeStruct((count, width), BF...]
where the time goes in v3:
time: 67.1 us; the launch traced here: 66.9 us
  Pallas kernels  66.2 us (99%)
    pallas_call x1, Pallas kernels, on_device(): pl.pallas_call(kernel, out_shape=(jax.ShapeDtypeStruct((count, width), BF...  64.4 us
    pallas_call x1, Pallas kernels, on_device(): pl.pallas_call(finish, out_shape=tuple((jax.ShapeDtypeStruct(result.shape...  1.79 us

profile of v3, /device:TPU:1, one launch (start us, length us, event | category | flops | bytes accessed | tf_op | source)
XLA Modules:
  0.0 66.9 jit_solution(5325162285296879356)
XLA Ops:
  0.6 64.4 %experts.1 = (bf16[128,512]{1,0:T(8,128)(2,1)}, f32[1,176,128]{2,1,0:T(8,128)}, f32[1,176,128]{2,1,0:T(8,128)}, f32[1,176,128]{2,1,0:T(8,128)}) custom-call(bf16[128,2048]{1,0:T(8,128)(2,1)} %tok_hbm.1, bf16[128,2048]{1,0:T(8,128)(2,1)} %grad_hbm.1, s32[2,128]{1,0:T(2,128)} %bitcast.2, f32[2,128]{1,0:T(2,128)} %bitcast.3, bf16[1,176,128]{2,1,0:T(8,128)(2,1)} %gate_hbm.1, ...), custom_call_target="tpu_custom_call" | custom-call | flops 2300000000 | bytes 4000000 | tf_op jit(solution)/shard_map/experts/pallas_call | solution.py:535
  65.1 1.8 %finish.1 = (bf16[128,512]{1,0:T(8,128)(2,1)}, f32[1,176,128]{2,1,0:T(8,128)}, f32[1,176,128]{2,1,0:T(8,128)}, f32[1,176,128]{2,1,0:T(8,128)}) custom-call(bf16[128,512]{1,0:T(8,128)(2,1)} %get-tuple-element.8.tok_ref, f32[1,176,128]{2,1,0:T(8,128)} %get-tuple-element.9.gate_ref, f32[1,176,128]{2,1,0:T(8,128)} %get-tuple-element.10.up_ref, ...), custom_call_target="tpu_custom_call" | custom-call | tf_op jit(solution)/shard_map/finish/pallas_call | solution.py:593

commit v4 on v3

--- a/solution.py
+++ b/solution.py
@@ -17,8 +17,8 @@
 NEAR = (6, 7)
 SPLIT = (1, 2, 3, 4)
 LAST_FAR = 5
-BATCHES = ((0, 3), (3, 5), (5, 6), (6, 8))
-GROUPS = ((1, 3),)
+BATCHES = ((0, 3), (3, 5), (5, 8))
+GROUPS = ((1, 3), (3, 5))
 CAP = 48
 HID = 176
 HID3 = 3 * HID
@@ -26,6 +26,22 @@
 PIECES = ((0, 144), (144, 128), (272, 128), (400, 128))
 
 
+SENDS = 36
+RECVS = 124
+
+
+class Numbered:
+    def __init__(self, sems, table, kind):
+        self.sems, self.table, self.kind = sems, table, kind
+
+    @property
+    def at(self):
+        return self
+
+    def __getitem__(self, key):
+        return self.sems.at[self.table.setdefault((self.kind, key), len(self.table))]
+
+
 def dot(a, b, ca, cb):
     return lax.dot_general(a, b, (((ca,), (cb,)), ((), ())), preferred_element_type=F32)
 
@@ -35,8 +51,11 @@
     tok_out, gate_out, up_out, down_out,
     tokq, gradq, tokf, gradf, routes_ref, gates_ref, pack, sendq, sendf, rows, weights, back_a, back_b, hid_a, hid_b,
     row_grad, wacc, wgrad, sib_rs, ring_in, ring_out, xs_in, gr_in, gx_in, yback, ret,
-    loc, y_s, y_r, x_s, x_r, ag_s, ag_r, sg_s, sg_r, xs_s, xs_r, gs_s, gs_r, yb_s, yb_r, sr_s, sr_r, rr_s, rr_r,
+    loc, send_sems, recv_sems,
 ):
+    table = {}
+    kinds = [Numbered(recv_sems, table, kind) for kind in range(9)]
+    y_r, x_r, ag_r, sg_r, xs_r, gs_r, yb_r, sr_r, rr_r = kinds
     d, e, m = lax.axis_index("dp"), lax.axis_index("expert"), lax.axis_index("mp")
     z, c = d // 2, d % 2
     width = tokq.shape[1]
@@ -51,7 +70,6 @@
         return (d, e, (m + shift) % 4)
 
     z_right, z_left, sibling = at_z(1), at_z(7), at_z(0, 1 - c)
-    z_right2, z_left2 = at_z(2), at_z(6)
     x_right, x_left, x_far = at_x(1), at_x(3), at_x(2)
 
     def quarter(shift):
@@ -65,18 +83,27 @@
             src_ref=src, dst_ref=dst, send_sem=send, recv_sem=recv, device_id=device, device_id_type=MESH
         )
 
-    pending = []
-
-    def send(src, dst, send_sem, recv_sem, device):
-        copy = remote(src, dst, send_sem, recv_sem, device)
+    pending, free = [], list(range(SENDS))
+
+    def drain(newest):
+        while len(pending) > newest:
+            copy, index = pending.pop(0)
+            copy.wait_send()
+            free.append(index)
+
+    def send(src, dst, recv_sem, device):
+        if not free:
+            drain(SENDS - 1)
+        index = free.pop(0)
+        copy = remote(src, dst, send_sems.at[index], recv_sem, device)
         copy.start()
-        pending.append(copy)
-
-    def arrived(dst, send_sem, recv_sem, device):
-        remote(dst, dst, send_sem, recv_sem, device).wait_recv()
+        pending.append((copy, index))
+
+    def arrived(dst, recv_sem, device):
+        remote(dst, dst, send_sems.at[0], recv_sem, device).wait_recv()
 
     barrier = pltpu.get_barrier_semaphore()
-    partners = [z_right, z_left, z_right2, z_left2, sibling, x_right, x_left, x_far] + [at_y(k) for k in range(1, 8)]
+    partners = [z_right, z_left, sibling, x_right, x_left, x_far] + [at_y(k) for k in range(1, 8)]
     for partner in partners:
         pl.semaphore_signal(barrier, inc=1, device_id=partner, device_id_type=MESH)
 
@@ -131,31 +158,31 @@
 
     def y_send(j, part=0, span=both):
         if j in NEAR:
-            send(sendf.at[j - FAR], rows.at[j], y_s.at[j, 0], y_r.at[j, 0], at_y(SHIFTS[j]))
+            send(sendf.at[j - FAR], rows.at[j], y_r.at[j, 0], at_y(SHIFTS[j]))
         else:
             send(
-                sendq.at[j - 1, span], rows.at[j, span, quarter(0)], y_s.at[j, part], y_r.at[j, part], at_y(SHIFTS[j]),
+                sendq.at[j - 1, span], rows.at[j, span, quarter(0)], y_r.at[j, part], at_y(SHIFTS[j]),
             )
 
     def y_arrived(j, part=0, span=both):
         where = rows.at[j] if j in NEAR else rows.at[j, span, quarter(0)]
-        arrived(where, y_s.at[j, part], y_r.at[j, part], at_y(8 - SHIFTS[j]))
+        arrived(where, y_r.at[j, part], at_y(8 - SHIFTS[j]))
 
     def x_send(j, part=0, span=both):
         block_out = rows.at[j, span, quarter(0)]
-        send(block_out, block_out, x_s.at[j - 1, part, 0], x_r.at[j - 1, part, 0], x_right)
-        send(block_out, block_out, x_s.at[j - 1, part, 1], x_r.at[j - 1, part, 1], x_left)
+        send(block_out, block_out, x_r.at[j - 1, part, 0], x_right)
+        send(block_out, block_out, x_r.at[j - 1, part, 1], x_left)
         if j == LAST_FAR:
-            send(block_out, block_out, x_s.at[j - 1, part, 2], x_r.at[j - 1, part, 2], x_far)
+            send(block_out, block_out, x_r.at[j - 1, part, 2], x_far)
 
     def x_arrived(j, side, part=0, span=both):
         shift, device = ((3, x_left), (1, x_right), (2, x_far))[side]
-        arrived(rows.at[j, span, quarter(shift)], x_s.at[j - 1, part, side], x_r.at[j - 1, part, side], device)
+        arrived(rows.at[j, span, quarter(shift)], x_r.at[j - 1, part, side], device)
 
     def forward_send(j, side):
         block_out = rows.at[j, grad_rows if side else token_rows, quarter(1 if side else 3)]
         device = x_left if side else x_right
-        send(block_out, block_out, x_s.at[j - 1, side, 2], x_r.at[j - 1, side, 2], device)
+        send(block_out, block_out, x_r.at[j - 1, side, 2], device)
 
     def x_forward(j, side):
         if j in SPLIT:
@@ -172,8 +199,8 @@
         if j in SPLIT:
             x_arrived(j, 1, 0, token_rows)
             x_arrived(j, 0, 1, grad_rows)
-        arrived(rows.at[j, token_rows, quarter(2)], x_s.at[j - 1, 0, 2], x_r.at[j - 1, 0, 2], x_left)
-        arrived(rows.at[j, grad_rows, quarter(2)], x_s.at[j - 1, 1, 2], x_r.at[j - 1, 1, 2], x_right)
+        arrived(rows.at[j, token_rows, quarter(2)], x_r.at[j - 1, 0, 2], x_left)
+        arrived(rows.at[j, grad_rows, quarter(2)], x_r.at[j - 1, 1, 2], x_right)
 
     def weight_part(shift, core, half):
         if half is None:
@@ -189,7 +216,7 @@
     def ag_send(step, side, half):
         part = weight_part(ag_shift(step - 1, side), c, half)
         device = z_right if side == 0 else z_left
-        send(part, part, ag_s.at[side, step - 1, half], ag_r.at[side, step - 1, half], device)
+        send(part, part, ag_r.at[side, step - 1, half], device)
 
     def sib_half(step, side):
         return side if step == 4 else None
@@ -197,7 +224,7 @@
     def sib_send(step, side):
         index = 1 + 2 * (step - 1) + side if step else 0
         part = weight_part(ag_shift(step, side), c, sib_half(step, side))
-        send(part, part, sg_s.at[index], sg_r.at[index], sibling)
+        send(part, part, sg_r.at[index], sibling)
 
     def ag_start():
         for copy in loads[4:7]:
@@ -212,8 +239,7 @@
             for side in (0, 1):
                 if half in ag_halves(step, side):
                     arrived(
-                        weight_part(ag_shift(step, side), c, half), ag_s.at[side, step - 1, half],
-                        ag_r.at[side, step - 1, half], z_left if side == 0 else z_right,
+                        weight_part(ag_shift(step, side), c, half), ag_r.at[side, step - 1, half], z_left if side == 0 else z_right,
                     )
                     if step < 4 and half in ag_halves(step + 1, side):
                         ag_send(step + 1, side, half)
@@ -221,12 +247,12 @@
             sib_send(step, side)
 
     def weights_complete():
-        arrived(weight_part(0, 1 - c, None), sg_s.at[0], sg_r.at[0], sibling)
+        arrived(weight_part(0, 1 - c, None), sg_r.at[0], sibling)
         for step in range(1, 5):
             for side in (0, 1):
                 index = 1 + 2 * (step - 1) + side
                 part = weight_part(ag_shift(step, side), 1 - c, sib_half(step, side))
-                arrived(part, sg_s.at[index], sg_r.at[index], sibling)
+                arrived(part, sg_r.at[index], sibling)
 
     def hidden_terms(b):
         first, last = BATCHES[b]
@@ -262,19 +288,19 @@
     def rs_send(j):
         for index, (shift, device) in enumerate(((1, x_right), (3, x_left), (2, x_far))):
             send(
-                row_grad.at[j, :, quarter(shift)], xs_in.at[j, index], xs_s.at[j, index], xs_r.at[j, index], device,
+                row_grad.at[j, :, quarter(shift)], xs_in.at[j, index], xs_r.at[j, index], device,
             )
 
     def rs_finish(j):
         total = row_grad[j, :, quarter(0)].astype(F32)
         for index, device in enumerate((x_left, x_right, x_far)):
-            arrived(xs_in.at[j, index], xs_s.at[j, index], xs_r.at[j, index], device)
+            arrived(xs_in.at[j, index], xs_r.at[j, index], device)
             total = total + xs_in[j, index].astype(F32)
         if j == 0:
             ret[0] = total.astype(BF16)
         else:
             yback[j] = total.astype(BF16)
-            send(yback.at[j], ret.at[j], yb_s.at[j], yb_r.at[j], at_y(8 - SHIFTS[j]))
+            send(yback.at[j], ret.at[j], yb_r.at[j], at_y(8 - SHIFTS[j]))
 
     def half_quarter(shift, side):
         return pl.ds(pl.multiple_of(((m + shift) % 4) * width + side * (width // 2), width // 2), width // 2)
@@ -284,30 +310,30 @@
         for side, device in enumerate((x_right, x_left)):
             send(
                 row_grad.at[first:last, :, half_quarter(2, side)], gr_in.at[side, first:last],
-                gs_s.at[g, side], gs_r.at[g, side], device,
+                gs_r.at[g, side], device,
             )
 
     def group_pass(g):
         first, last = GROUPS[g]
         for side, (shift, device, source) in enumerate(((1, x_right, x_left), (3, x_left, x_right))):
-            arrived(gr_in.at[side, first:last], gs_s.at[g, side], gs_r.at[g, side], source)
+            arrived(gr_in.at[side, first:last], gs_r.at[g, side], source)
             lanes = half_quarter(shift, side)
             for j in range(first, last):
                 total = row_grad[j, :, lanes].astype(F32) + gr_in[side, j].astype(F32)
                 row_grad[j, :, lanes] = total.astype(BF16)
             send(
                 row_grad.at[first:last, :, quarter(shift)], gx_in.at[side, first:last],
-                gs_s.at[g, 2 + side], gs_r.at[g, 2 + side], device,
+                gs_r.at[g, 2 + side], device,
             )
 
     def group_finish(g):
         first, last = GROUPS[g]
         for side, source in enumerate((x_left, x_right)):
-            arrived(gx_in.at[side, first:last], gs_s.at[g, 2 + side], gs_r.at[g, 2 + side], source)
+            arrived(gx_in.at[side, first:last], gs_r.at[g, 2 + side], source)
         for j in range(first, last):
             total = row_grad[j, :, quarter(0)].astype(F32) + gx_in[0, j].astype(F32) + gx_in[1, j].astype(F32)
             yback[j] = total.astype(BF16)
-            send(yback.at[j], ret.at[j], yb_s.at[j], yb_r.at[j], at_y(8 - SHIFTS[j]))
+            send(yback.at[j], ret.at[j], yb_r.at[j], at_y(8 - SHIFTS[j]))
 
     def weight_early():
         first, last = BATCHES[0]
@@ -324,71 +350,64 @@
         grad_d = wacc[2 * HID : HID3, lanes] + dot(hid_b[...], batch(first, last, CAP, lanes), 1, 0)
         wgrad[0 : 2 * HID, lanes] = grad_gu.astype(BF16)
         wgrad[2 * HID : HID3, lanes] = grad_d.astype(BF16)
-        send(wgrad.at[:, block(shift, 1 - c)], sib_rs.at[index], sr_s.at[index], sr_r.at[index], sibling)
+        send(wgrad.at[:, block(shift, 1 - c)], sib_rs.at[index], sr_r.at[index], sibling)
 
     chunk_shifts = (4, 3, 5, 2, 6, 1, 7, 0)
 
     def pair_ready(index):
-        arrived(sib_rs.at[index], sr_s.at[index], sr_r.at[index], sibling)
+        arrived(sib_rs.at[index], sr_r.at[index], sibling)
 
     def pair_sum(index, lo, size):
         mine = wgrad[pl.ds(lo, size), block(chunk_shifts[index], c)].astype(F32)
         return mine + sib_rs[index, pl.ds(lo, size), :].astype(F32)
 
-    def ring_part(ref, side, slot, piece):
-        return ref.at[side, slot, pl.ds(*PIECES[piece])]
-
-    def ring_send(side, slot, piece, total):
+    def ring_part(ref, side, step, piece):
+        return ref.at[side, step - 1, pl.ds(*PIECES[piece])]
+
+    def ring_send(side, step, piece, total):
         lo, size = PIECES[piece]
-        ring_out[side, slot, pl.ds(lo, size), :] = total.astype(BF16)
+        ring_out[side, step - 1, pl.ds(lo, size), :] = total.astype(BF16)
         send(
-            ring_part(ring_out, side, slot, piece), ring_part(ring_in, side, slot, piece),
-            rr_s.at[side, slot, piece], rr_r.at[side, slot, piece],
-            ((z_right, z_left), (z_right2, z_left2))[slot == 0][side],
+            ring_part(ring_out, side, step, piece), ring_part(ring_in, side, step, piece),
+            rr_r.at[side, step - 1, piece], (z_right, z_left)[side],
         )
 
-    def ring_recv(side, slot, piece):
+    def ring_recv(side, step, piece):
         lo, size = PIECES[piece]
         arrived(
-            ring_part(ring_in, side, slot, piece), rr_s.at[side, slot, piece], rr_r.at[side, slot, piece],
-            ((z_left, z_right), (z_left2, z_right2))[slot == 0][side],
+            ring_part(ring_in, side, step, piece), rr_r.at[side, step - 1, piece],
+            (z_left, z_right)[side],
         )
-        return ring_in[side, slot, pl.ds(lo, size), :].astype(F32)
-
-    def ring_order():
-        for turn in range(4):
-            for side in (0, 1):
-                yield side, (turn + 2 * (1 - side)) % 4
-
-    def ring_far():
+        return ring_in[side, step - 1, pl.ds(lo, size), :].astype(F32)
+
+    def ring_first():
         pair_ready(0)
         for turn in (0, 1):
             for side in (0, 1):
                 piece = 2 * side + turn
-                ring_send(side, 0, piece, pair_sum(0, *PIECES[piece]))
-
-    def ring_first():
-        for side in (0, 1):
-            pair_ready(1 + side)
-        for side, piece in ring_order():
-            ring_send(side, 1, piece, pair_sum(1 + side, *PIECES[piece]))
-
-    def ring_step(slot, half):
-        if half == 0:
+                ring_send(side, 1, piece, pair_sum(0, *PIECES[piece]))
+
+    paired = set()
+
+    def ring_step(step, half):
+        if step not in paired:
+            paired.add(step)
             for side in (0, 1):
-                pair_ready(2 * slot - 1 + side)
-        for side, piece in tuple(ring_order())[4 * half : 4 * half + 4]:
-            total = pair_sum(2 * slot - 1 + side, *PIECES[piece]) + ring_recv(side, slot - 1, piece)
-            if slot == 2 and piece // 2 == side:
-                total = total + ring_recv(side, 0, piece)
-            ring_send(side, slot, piece, total)
+                pair_ready(2 * step - 3 + side)
+        for turn in (2 * half, 2 * half + 1):
+            for side in (0, 1):
+                piece = (turn + 2 * side) % 4
+                total = pair_sum(2 * step - 3 + side, *PIECES[piece])
+                if step > 2 or piece // 2 == side:
+                    total = total + ring_recv(side, step - 1, piece)
+                ring_send(side, step, piece, total)
 
     def weight_outputs():
         pair_ready(7)
         outs = ((0, HID, gate_out), (HID, 2 * HID, up_out), (2 * HID, HID3, down_out))
         for piece in range(4):
             lo, size = PIECES[piece]
-            total = pair_sum(7, lo, size) + ring_recv(0, 3, piece) + ring_recv(1, 3, piece)
+            total = pair_sum(7, lo, size) + ring_recv(0, 4, piece) + ring_recv(1, 4, piece)
             for first, last, out in outs:
                 start, stop = max(first, lo), min(last, lo + size)
                 if start < stop:
@@ -396,7 +415,7 @@
 
     def token_outputs():
         for j in range(1, SLOTS):
-            arrived(ret.at[j], yb_s.at[j], yb_r.at[j], at_y(SHIFTS[j]))
+            arrived(ret.at[j], yb_r.at[j], at_y(SHIFTS[j]))
         back_rows = ret[...].reshape(SLOTS * CAP, width)
         tok_out[...] = dot(pack[...], back_rows, 0, 0).astype(BF16)
 
@@ -420,101 +439,100 @@
     pack_quarter(1, 3)
     pl.semaphore_wait(barrier, len(partners))
 
+    y_send(2, 1, grad_rows)
     y_send(1, 1, grad_rows)
+    ag_start()
+    pack_quarter(3, FAR)
     y_send(2, 0, token_rows)
     y_send(1, 0, token_rows)
-    ag_start()
-    pack_quarter(3, FAR)
+    y_send(3, 1, grad_rows)
+    y_send(4, 1, grad_rows)
+    ag_step(1)
+    y_send(3, 0, token_rows)
+    y_arrived(1, 1, grad_rows)
+    x_send(1, 1, grad_rows)
     pack_full()
-    y_send(2, 1, grad_rows)
-    y_send(4, 1, grad_rows)
+    y_arrived(2, 1, grad_rows)
+    x_send(2, 1, grad_rows)
     y_send(4, 0, token_rows)
-    y_send(3, 0, token_rows)
+    y_arrived(1, 0, token_rows)
+    x_send(1, 0, token_rows)
     y_arrived(2, 0, token_rows)
     x_send(2, 0, token_rows)
-    ag_step(1)
-    y_send(3, 1, grad_rows)
+    ag_step(2)
+    y_arrived(4, 1, grad_rows)
+    x_send(4, 1, grad_rows)
     y_send(5)
-    y_arrived(1, 1, grad_rows)
-    x_send(1, 1, grad_rows)
-    y_arrived(1, 0, token_rows)
-    x_send(1, 0, token_rows)
-    y_send(7)
-    y_arrived(2, 1, grad_rows)
-    x_send(2, 1, grad_rows)
+    y_arrived(3, 1, grad_rows)
+    x_send(3, 1, grad_rows)
+    x_forward(1, 0)
+    x_forward(1, 1)
+    y_arrived(4, 0, token_rows)
+    x_send(4, 0, token_rows)
     y_arrived(3, 0, token_rows)
     x_send(3, 0, token_rows)
-    y_arrived(4, 1, grad_rows)
-    x_send(4, 1, grad_rows)
-    ag_step(2)
+    y_send(7)
+    ag_step(3)
+    y_send(6)
     x_forward(2, 1)
-    x_forward(1, 0)
-    y_send(6)
-    y_arrived(3, 1, grad_rows)
-    x_send(3, 1, grad_rows)
-    y_arrived(4, 0, token_rows)
-    x_send(4, 0, token_rows)
+    x_forward(2, 0)
+    x_forward(3, 1)
     x_forward(4, 1)
-    x_forward(2, 0)
-    ag_step(3)
+    x_forward(4, 0)
+    x_complete(1)
     x_forward(3, 0)
-    x_forward(1, 1)
-    x_forward(3, 1)
-    x_forward(4, 0)
     y_arrived(5)
     x_send(5)
-    x_complete(1)
     x_complete(2)
     ag_step(4)
     weights_complete()
+    x_complete(4)
+    forward(0)
     x_complete(3)
-    forward(0)
-    x_complete(4)
+    forward(1)
+    row_grads(1)
+    group_start(1)
+    weight_early()
     row_grads(0)
     group_start(0)
-    forward(1)
-    row_grads(1)
-    rs_send(3)
-    weight_early()
     y_arrived(7)
     y_arrived(6)
-    forward(3)
-    rs_send(4)
     x_complete(5)
     forward(2)
+    row_grads(2)
+    rs_send(5)
     weight_chunk(0)
-    row_grads(2)
-    group_pass(0)
     weight_chunk(1)
     weight_chunk(2)
-    ring_far()
-    rs_send(5)
+    weight_chunk(3)
+    group_pass(0)
     ring_first()
-    row_grads(3)
-    rs_finish(3)
-    weight_chunk(3)
-    rs_send(7)
-    rs_send(6)
-    rs_finish(4)
-    rs_send(0)
     weight_chunk(4)
     weight_chunk(5)
+    ring_step(2, 1)
+    group_pass(1)
+    rs_send(6)
+    rs_send(7)
+    ring_step(2, 0)
+    rs_finish(5)
+    ring_step(3, 1)
     group_finish(0)
+    ring_step(3, 0)
     weight_chunk(6)
+    group_finish(1)
+    rs_send(0)
+    ring_step(4, 1)
+    ring_step(4, 0)
     weight_chunk(7)
-    ring_step(2, 0)
-    ring_step(2, 1)
-    rs_finish(5)
-    ring_step(3, 0)
+    rs_finish(6)
     rs_finish(7)
-    ring_step(3, 1)
-    rs_finish(6)
     rs_finish(0)
+    drain(24)
     weight_outputs()
+    drain(0)
     token_outputs()
 
-    for copy in pending:
-        copy.wait_send()
+    drain(0)
 
 
 def finish(tok_ref, gate_ref, up_ref, down_ref, tok_out, gate_out, up_out, down_out):
@@ -565,24 +583,8 @@
             pltpu.VMEM((SLOTS, CAP, width), BF16),
             pltpu.VMEM((SLOTS, CAP, width), BF16),
             sems((9,)),
-            sems((FAR + len(NEAR), 2)),
-            sems((FAR + len(NEAR), 2)),
-            sems((FAR - 1, 2, 3)),
-            sems((FAR - 1, 2, 3)),
-            sems((2, 4, 2)),
-            sems((2, 4, 2)),
-            sems((9,)),
-            sems((9,)),
-            sems((SLOTS, 3)),
-            sems((SLOTS, 3)),
-            sems((len(GROUPS), 4)),
-            sems((len(GROUPS), 4)),
-            sems((SLOTS,)),
-            sems((SLOTS,)),
-            sems((8,)),
-            sems((8,)),
-            sems((2, 4, 4)),
-            sems((2, 4, 4)),
+            sems((SENDS,)),
+            sems((RECVS,)),
         ],
         compiler_params=pltpu.CompilerParams(
             collective_id=0, has_side_effects=True, vmem_limit_bytes=56 * 1024 * 1024

time: 67.1 us -> 65 us (0.969)
  Pallas kernels: 66.2 us -> 64.2 us
    pallas_call x1, Pallas kernels: 64.4 us -> 62.4 us  [on_device(): pl.pallas_call(kernel, out_shape=(jax.ShapeDtypeStruct((count, width), BF...]
where the time goes in v4:
time: 65 us; the launch traced here: 64.8 us
  Pallas kernels  64.2 us (99%)
    pallas_call x1, Pallas kernels, on_device(): pl.pallas_call(kernel, out_shape=(jax.ShapeDtypeStruct((count, width), BF...  62.4 us
    pallas_call x1, Pallas kernels, on_device(): pl.pallas_call(finish, out_shape=tuple((jax.ShapeDtypeStruct(result.shape...  1.79 us

profile of v4, /device:TPU:1, one launch (start us, length us, event | category | flops | bytes accessed | tf_op | source)
XLA Modules:
  0.0 64.8 jit_solution(10355224989977585995)
XLA Ops:
  0.6 62.4 %experts.1 = (bf16[128,512]{1,0:T(8,128)(2,1)}, f32[1,176,128]{2,1,0:T(8,128)}, f32[1,176,128]{2,1,0:T(8,128)}, f32[1,176,128]{2,1,0:T(8,128)}) custom-call(bf16[128,2048]{1,0:T(8,128)(2,1)} %tok_hbm.1, bf16[128,2048]{1,0:T(8,128)(2,1)} %grad_hbm.1, s32[2,128]{1,0:T(2,128)} %bitcast.2, f32[2,128]{1,0:T(2,128)} %bitcast.3, bf16[1,176,128]{2,1,0:T(8,128)(2,1)} %gate_hbm.1, ...), custom_call_target="tpu_custom_call" | custom-call | flops 2300000000 | bytes 4000000 | tf_op jit(solution)/shard_map/experts/pallas_call | solution.py:553
  63.0 1.8 %finish.1 = (bf16[128,512]{1,0:T(8,128)(2,1)}, f32[1,176,128]{2,1,0:T(8,128)}, f32[1,176,128]{2,1,0:T(8,128)}, f32[1,176,128]{2,1,0:T(8,128)}) custom-call(bf16[128,512]{1,0:T(8,128)(2,1)} %get-tuple-element.8.tok_ref, f32[1,176,128]{2,1,0:T(8,128)} %get-tuple-element.9.gate_ref, f32[1,176,128]{2,1,0:T(8,128)} %get-tuple-element.10.up_ref, ...), custom_call_target="tpu_custom_call" | custom-call | tf_op jit(solution)/shard_map/finish/pallas_call | solution.py:595

commit v5 on v4

--- a/solution.py
+++ b/solution.py
@@ -23,11 +23,13 @@
 HID = 176
 HID3 = 3 * HID
 HALVES = ((0, 272), (272, 256))
-PIECES = ((0, 144), (144, 128), (272, 128), (400, 128))
-
-
-SENDS = 36
-RECVS = 124
+PIECES = HALVES
+
+
+SENDS = 24
+RECVS = 69
+
+PART = len(PIECES) // 2
 
 
 class Numbered:
@@ -168,39 +170,33 @@
         where = rows.at[j] if j in NEAR else rows.at[j, span, quarter(0)]
         arrived(where, y_r.at[j, part], at_y(8 - SHIFTS[j]))
 
+    def x_sem(j, part, side):
+        late = j == LAST_FAR or side != part
+        return x_r.at[j - 1, 2 if late else part]
+
     def x_send(j, part=0, span=both):
         block_out = rows.at[j, span, quarter(0)]
-        send(block_out, block_out, x_r.at[j - 1, part, 0], x_right)
-        send(block_out, block_out, x_r.at[j - 1, part, 1], x_left)
+        send(block_out, block_out, x_sem(j, part, 0), x_right)
+        send(block_out, block_out, x_sem(j, part, 1), x_left)
         if j == LAST_FAR:
-            send(block_out, block_out, x_r.at[j - 1, part, 2], x_far)
+            send(block_out, block_out, x_sem(j, part, 2), x_far)
 
     def x_arrived(j, side, part=0, span=both):
         shift, device = ((3, x_left), (1, x_right), (2, x_far))[side]
-        arrived(rows.at[j, span, quarter(shift)], x_r.at[j - 1, part, side], device)
+        arrived(rows.at[j, span, quarter(shift)], x_sem(j, part, side), device)
 
     def forward_send(j, side):
         block_out = rows.at[j, grad_rows if side else token_rows, quarter(1 if side else 3)]
         device = x_left if side else x_right
-        send(block_out, block_out, x_r.at[j - 1, side, 2], device)
+        send(block_out, block_out, x_sem(j, side, 2), device)
 
     def x_forward(j, side):
-        if j in SPLIT:
-            x_arrived(j, side, side, (token_rows, grad_rows)[side])
-        else:
-            x_arrived(j, side)
+        x_arrived(j, side, side, (token_rows, grad_rows)[side])
         forward_send(j, side)
 
     def x_complete(j):
-        if j == LAST_FAR:
-            for side in (0, 1, 2):
-                x_arrived(j, side)
-            return
-        if j in SPLIT:
-            x_arrived(j, 1, 0, token_rows)
-            x_arrived(j, 0, 1, grad_rows)
-        arrived(rows.at[j, token_rows, quarter(2)], x_r.at[j - 1, 0, 2], x_left)
-        arrived(rows.at[j, grad_rows, quarter(2)], x_r.at[j - 1, 1, 2], x_right)
+        span = pl.ds(0, (3 if j == LAST_FAR else 2) * width)
+        arrived(rows.at[j, :, span], x_sem(j, 0, 2), x_left)
 
     def weight_part(shift, core, half):
         if half is None:
@@ -222,9 +218,8 @@
         return side if step == 4 else None
 
     def sib_send(step, side):
-        index = 1 + 2 * (step - 1) + side if step else 0
         part = weight_part(ag_shift(step, side), c, sib_half(step, side))
-        send(part, part, sg_r.at[index], sibling)
+        send(part, part, sg_r.at[0], sibling)
 
     def ag_start():
         for copy in loads[4:7]:
@@ -247,12 +242,7 @@
             sib_send(step, side)
 
     def weights_complete():
-        arrived(weight_part(0, 1 - c, None), sg_r.at[0], sibling)
-        for step in range(1, 5):
-            for side in (0, 1):
-                index = 1 + 2 * (step - 1) + side
-                part = weight_part(ag_shift(step, side), 1 - c, sib_half(step, side))
-                arrived(part, sg_r.at[index], sibling)
+        arrived(weights.at[:, pl.ds(0, weights.shape[1] // 2)], sg_r.at[0], sibling)
 
     def hidden_terms(b):
         first, last = BATCHES[b]
@@ -288,19 +278,19 @@
     def rs_send(j):
         for index, (shift, device) in enumerate(((1, x_right), (3, x_left), (2, x_far))):
             send(
-                row_grad.at[j, :, quarter(shift)], xs_in.at[j, index], xs_r.at[j, index], device,
+                row_grad.at[j, :, quarter(shift)], xs_in.at[j, index], xs_r.at[j], device,
             )
 
     def rs_finish(j):
+        arrived(xs_in.at[j], xs_r.at[j], x_far)
         total = row_grad[j, :, quarter(0)].astype(F32)
-        for index, device in enumerate((x_left, x_right, x_far)):
-            arrived(xs_in.at[j, index], xs_r.at[j, index], device)
+        for index in range(3):
             total = total + xs_in[j, index].astype(F32)
         if j == 0:
             ret[0] = total.astype(BF16)
         else:
             yback[j] = total.astype(BF16)
-            send(yback.at[j], ret.at[j], yb_r.at[j], at_y(8 - SHIFTS[j]))
+            send(yback.at[j], ret.at[j], yb_r.at[0], at_y(8 - SHIFTS[j]))
 
     def half_quarter(shift, side):
         return pl.ds(pl.multiple_of(((m + shift) % 4) * width + side * (width // 2), width // 2), width // 2)
@@ -323,17 +313,16 @@
                 row_grad[j, :, lanes] = total.astype(BF16)
             send(
                 row_grad.at[first:last, :, quarter(shift)], gx_in.at[side, first:last],
-                gs_r.at[g, 2 + side], device,
+                gs_r.at[g, 2], device,
             )
 
     def group_finish(g):
         first, last = GROUPS[g]
-        for side, source in enumerate((x_left, x_right)):
-            arrived(gx_in.at[side, first:last], gs_r.at[g, 2 + side], source)
+        arrived(gx_in.at[:, first:last], gs_r.at[g, 2], x_left)
         for j in range(first, last):
             total = row_grad[j, :, quarter(0)].astype(F32) + gx_in[0, j].astype(F32) + gx_in[1, j].astype(F32)
             yback[j] = total.astype(BF16)
-            send(yback.at[j], ret.at[j], yb_r.at[j], at_y(8 - SHIFTS[j]))
+            send(yback.at[j], ret.at[j], yb_r.at[0], at_y(8 - SHIFTS[j]))
 
     def weight_early():
         first, last = BATCHES[0]
@@ -350,12 +339,12 @@
         grad_d = wacc[2 * HID : HID3, lanes] + dot(hid_b[...], batch(first, last, CAP, lanes), 1, 0)
         wgrad[0 : 2 * HID, lanes] = grad_gu.astype(BF16)
         wgrad[2 * HID : HID3, lanes] = grad_d.astype(BF16)
-        send(wgrad.at[:, block(shift, 1 - c)], sib_rs.at[index], sr_r.at[index], sibling)
+        send(wgrad.at[:, block(shift, 1 - c)], sib_rs.at[index], sr_r.at[(index + 1) // 2], sibling)
 
     chunk_shifts = (4, 3, 5, 2, 6, 1, 7, 0)
 
     def pair_ready(index):
-        arrived(sib_rs.at[index], sr_r.at[index], sibling)
+        arrived(sib_rs.at[index], sr_r.at[(index + 1) // 2], sibling)
 
     def pair_sum(index, lo, size):
         mine = wgrad[pl.ds(lo, size), block(chunk_shifts[index], c)].astype(F32)
@@ -382,9 +371,9 @@
 
     def ring_first():
         pair_ready(0)
-        for turn in (0, 1):
+        for turn in range(PART):
             for side in (0, 1):
-                piece = 2 * side + turn
+                piece = PART * side + turn
                 ring_send(side, 1, piece, pair_sum(0, *PIECES[piece]))
 
     paired = set()
@@ -392,20 +381,19 @@
     def ring_step(step, half):
         if step not in paired:
             paired.add(step)
+            arrived(sib_rs.at[2 * step - 3 : 2 * step - 1], sr_r.at[step - 1], sibling)
+        for turn in range(PART * half, PART * (half + 1)):
             for side in (0, 1):
-                pair_ready(2 * step - 3 + side)
-        for turn in (2 * half, 2 * half + 1):
-            for side in (0, 1):
-                piece = (turn + 2 * side) % 4
+                piece = (turn + PART * side) % len(PIECES)
                 total = pair_sum(2 * step - 3 + side, *PIECES[piece])
-                if step > 2 or piece // 2 == side:
+                if step > 2 or piece // PART == side:
                     total = total + ring_recv(side, step - 1, piece)
                 ring_send(side, step, piece, total)
 
     def weight_outputs():
         pair_ready(7)
         outs = ((0, HID, gate_out), (HID, 2 * HID, up_out), (2 * HID, HID3, down_out))
-        for piece in range(4):
+        for piece in range(len(PIECES)):
             lo, size = PIECES[piece]
             total = pair_sum(7, lo, size) + ring_recv(0, 4, piece) + ring_recv(1, 4, piece)
             for first, last, out in outs:
@@ -414,8 +402,7 @@
                     out[0, start - first : stop - first] = total[start - lo : stop - lo]
 
     def token_outputs():
-        for j in range(1, SLOTS):
-            arrived(ret.at[j], yb_r.at[j], at_y(SHIFTS[j]))
+        arrived(ret.at[1:SLOTS], yb_r.at[0], at_y(1))
         back_rows = ret[...].reshape(SLOTS * CAP, width)
         tok_out[...] = dot(pack[...], back_rows, 0, 0).astype(BF16)
 

time: 65 us -> 64.6 us (level)
  no operation moved by 1% of the time
where the time goes in v5:
time: 64.6 us; the launch traced here: 64.5 us
  Pallas kernels  63.8 us (99%)
    pallas_call x1, Pallas kernels, on_device(): pl.pallas_call(kernel, out_shape=(jax.ShapeDtypeStruct((count, width), BF...  62 us
    pallas_call x1, Pallas kernels, on_device(): pl.pallas_call(finish, out_shape=tuple((jax.ShapeDtypeStruct(result.shape...  1.79 us

profile of v5, /device:TPU:1, one launch (start us, length us, event | category | flops | bytes accessed | tf_op | source)
XLA Modules:
  0.0 64.5 jit_solution(9699451375357481349)
XLA Ops:
  0.6 62.0 %experts.1 = (bf16[128,512]{1,0:T(8,128)(2,1)}, f32[1,176,128]{2,1,0:T(8,128)}, f32[1,176,128]{2,1,0:T(8,128)}, f32[1,176,128]{2,1,0:T(8,128)}) custom-call(bf16[128,2048]{1,0:T(8,128)(2,1)} %tok_hbm.1, bf16[128,2048]{1,0:T(8,128)(2,1)} %grad_hbm.1, s32[2,128]{1,0:T(2,128)} %bitcast.2, f32[2,128]{1,0:T(2,128)} %bitcast.3, bf16[1,176,128]{2,1,0:T(8,128)(2,1)} %gate_hbm.1, ...), custom_call_target="tpu_custom_call" | custom-call | flops 2300000000 | bytes 4000000 | tf_op jit(solution)/shard_map/experts/pallas_call | solution.py:540
  62.7 1.8 %finish.1 = (bf16[128,512]{1,0:T(8,128)(2,1)}, f32[1,176,128]{2,1,0:T(8,128)}, f32[1,176,128]{2,1,0:T(8,128)}, f32[1,176,128]{2,1,0:T(8,128)}) custom-call(bf16[128,512]{1,0:T(8,128)(2,1)} %get-tuple-element.8.tok_ref, f32[1,176,128]{2,1,0:T(8,128)} %get-tuple-element.9.gate_ref, f32[1,176,128]{2,1,0:T(8,128)} %get-tuple-element.10.up_ref, ...), custom_call_target="tpu_custom_call" | custom-call | tf_op jit(solution)/shard_map/finish/pallas_call | solution.py:582
